TPU v7x, 1024 devices: a whole 4x4x32 slice. The times are simulated.
1024 devices in a mesh: win: 16 (over z_lo), tile: 64 (over y, x, z_hi, core).
Axes of the slice: x: 4, y: 4, z: 32 (z_hi: 2, z_lo: 16; z = z_hi * 16 + z_lo), core: 2. Of those that a mesh axis runs over, the one named last changes fastest.
Arguments:
- increment: float32 [16, 72, 384, 768], P('win', None, 'tile'), may hold values from -6 to 6
- background: float32 [72, 384, 768], P(None, 'tile'), may hold values from -6 to 6
- lat_diffusion: float32 [16, 384, 768], P('win', 'tile'), may hold values from 0.05 to 0.2
- lon_diffusion: float32 [16, 384, 768], P('win', 'tile'), may hold values from 0.1 to 0.2
- advection: float32 [16, 384, 768], P('win', 'tile'), may hold values from -0.4 to 0.4
- spectrum: float32 [512, 384], P('tile'), may hold values from 0.3 to 3
- obs_index: int32 [16, 32768], P('win', 'tile'), may hold values from 0 to 331775
- obs_count: int32 [16, 64], P('win', 'tile'), may hold values from 1 to 512, as said below
- innovation: float32 [16, 32768], P('win', 'tile'), may hold values from -6 to 6
- obs_precision: float32 [16, 32768], P('win', 'tile'), may hold values from 0.25 to 2
Outputs:
- gradient: float32 [16, 72, 384, 768], P('win', None, 'tile')
Inputs may be any that keep to these rules, and one draw needn't show every extreme that they name: `obs_index`: each entry is level * 6 * 768 + row * 768 + longitude, counted within the rows of its own tile. Only the first obs_count[w, t] slots of tile t's block of a sub-window are live; in every draw some tile of some sub-window has all 512 live.
All inputs are finite; a program needn't handle non-finite values.
Results may differ from a plain program's by a relative error of at most 0.000062.
Values sent between devices are 32-bit elements; how exact they have to be, the bound alone decides.
A program may use at most 32 MiB of HBM per device.

v0:
```python
import jax
import jax.numpy as jnp
from jax import lax
from jax.sharding import PartitionSpec as P


def with_halo(cells, sides, width):
    for axis, dim in sides:
        count = lax.axis_size(axis)
        ends = count - 1
        head = lax.slice_in_dim(cells, 0, width, axis=dim)
        tail = lax.slice_in_dim(cells, cells.shape[dim] - width, cells.shape[dim], axis=dim)
        cells = jnp.concatenate(
            [
                lax.ppermute(tail, axis, [(i, (i + 1) % count) for i in range(ends)]),
                cells,
                lax.ppermute(head, axis, [((i + 1) % count, i) for i in range(ends)]),
            ],
            axis=dim,
        )
    return cells


def passed_along(block, axis, distance):
    devices = range(lax.axis_size(axis))
    route = [(i - distance, i) for i in devices if i - distance in devices]
    return lax.ppermute(block, axis, route)


def longitude_basis(width, kept):
    half = kept // 2
    wave = jnp.arange(kept, dtype=jnp.int32)
    places = jnp.arange(width, dtype=jnp.int32)
    number = jnp.where(wave < half, wave, wave - half + 1)
    phase = number[:, None] * places[None, :] % width
    angle = 2.0 * jnp.pi * phase.astype(jnp.float32) / width
    scale = jnp.where(wave == 0, jnp.sqrt(1.0 / width), jnp.sqrt(2.0 / width)).astype(jnp.float32)
    table = jnp.where((wave < half)[:, None], jnp.cos(angle), jnp.sin(angle))
    return table * scale[:, None]


def latitude_basis(height):
    modes = jnp.arange(height, dtype=jnp.int32)
    phase = modes[:, None] * (2 * modes[None, :] + 1) % (4 * height)
    angle = jnp.pi * phase.astype(jnp.float32) / (2.0 * height)
    scale = jnp.where(modes == 0, jnp.sqrt(1.0 / height), jnp.sqrt(2.0 / height)).astype(
        jnp.float32
    )
    return jnp.cos(angle) * scale[:, None]


def tl_step(center, north, south, lat_coef, lon_coef, drift):
    east = jnp.roll(center, -1, axis=2)
    west = jnp.roll(center, 1, axis=2)
    return (
        (1.0 - 2.0 * lat_coef - 2.0 * lon_coef) * center
        + lat_coef * (north + south)
        + (lon_coef - 0.5 * drift) * east
        + (lon_coef + 0.5 * drift) * west
    )


def rows_halo(field):
    return with_halo(field, (("tile", 1),), 1)


def neighbour_window(field, offset):
    return passed_along(field, "win", offset)


def adjoint_step(field, lat_coef, lon_coef, drift):
    padded = rows_halo(lat_coef * field)
    eastward = (lon_coef - 0.5 * drift) * field
    westward = (lon_coef + 0.5 * drift) * field
    return (
        (1.0 - 2.0 * lat_coef - 2.0 * lon_coef) * field
        + padded[:, 2:]
        + padded[:, :-2]
        + jnp.roll(eastward, 1, axis=2)
        + jnp.roll(westward, -1, axis=2)
    )


def to_field(coefs, zonal, levels, row_count):
    grid = jnp.einsum("kx,km->mx", zonal, coefs, precision=lax.Precision.HIGHEST)
    return grid.reshape(levels, row_count, grid.shape[1])


def body(
    increment,
    background,
    lat_diffusion,
    lon_diffusion,
    advection,
    spectrum,
    obs_index,
    obs_count,
    innovation,
    obs_precision,
):
    highest = lax.Precision.HIGHEST
    state = increment[0]
    levels, row_count, longitudes = state.shape
    lat_coef = lat_diffusion[0]
    lon_coef = lon_diffusion[0]
    drift = advection[0]
    tiles = lax.axis_size("tile")
    height = row_count * tiles
    kept = 2 * (longitudes // 3)
    zonal = longitude_basis(longitudes, kept)
    merid = latitude_basis(height).reshape(height, tiles, row_count)
    propagated = state
    for repeat in range(2):
        padded = rows_halo(propagated)
        propagated = tl_step(propagated, padded[:, 2:], padded[:, :-2], lat_coef, lon_coef, drift)
    earlier = neighbour_window(propagated, 1)
    opening = lax.axis_index("win") == 0
    mismatch = state - jnp.where(opening, background, earlier)
    flat = mismatch.reshape(levels * row_count, longitudes)
    coefs = jnp.einsum("kx,mx->km", zonal, flat, precision=highest)
    modes_in = lax.all_to_all(coefs, "tile", split_axis=0, concat_axis=1, tiled=True)
    group = modes_in.shape[0]
    blocks = modes_in.reshape(group, tiles, levels, row_count)
    modal = jnp.einsum("ktlr,mtr->klm", blocks, merid, precision=highest) * spectrum[:, None, :]
    back = jnp.einsum("klm,mtr->ktlr", modal, merid, precision=highest)
    back = back.reshape(group, tiles * levels * row_count)
    grid_coefs = lax.all_to_all(back, "tile", split_axis=1, concat_axis=0, tiled=True)
    multiplier = to_field(grid_coefs, zonal, levels, row_count)
    later = neighbour_window(multiplier, -1)
    cells = obs_index[0]
    slots = jnp.arange(cells.shape[0], dtype=jnp.int32)
    live = slots < obs_count[0, 0]
    values = propagated.reshape(-1)[cells]
    departure = jnp.where(live, obs_precision[0] * (values - innovation[0]), jnp.zeros_like(values))
    placed = jnp.zeros((levels * row_count * longitudes,), jnp.float32).at[cells].add(departure)
    forcing = later - placed.reshape(levels, row_count, longitudes)
    adjoint = forcing
    for repeat in range(2):
        adjoint = adjoint_step(adjoint, lat_coef, lon_coef, drift)
    return (multiplier - adjoint)[None]


def solution(mesh):
    in_specs = (
        P("win", None, "tile", None),
        P(None, "tile", None),
        P("win", "tile", None),
        P("win", "tile", None),
        P("win", "tile", None),
        P("tile", None),
        P("win", "tile"),
        P("win", "tile"),
        P("win", "tile"),
        P("win", "tile"),
    )
    out_specs = P("win", None, "tile", None)
    return jax.shard_map(body, mesh=mesh, in_specs=in_specs, out_specs=out_specs, check_vma=False)
```

profile of v0, /device:TPU:152, one launch (start us, length us, event | category | flops | bytes accessed | tf_op | source)
XLA Modules:
  0.0 595.6 jit_solution(8942884414094684915)
XLA Ops:
  0.0 1.2 fusion.118
  1.2 26.0 %collective-permute-start = (f32[72,1,768]{2,0,1:T(8,128)S(1)}, f32[72,1,768]{2,0,1:T(8,128)S(1)}, u32[]{:S(2)}, u32[]{:S(2)}) collective-permute-start(f32[72,1,768]{2,0,1:T(8,128)S(1)} %get-tuple-element.27), channel_id=1, source_target_pairs={{1,0},{2,1},{3,2},{4,3},{5,4},{6,5},{7,6},{8,7},{9,8},{10,9},{11,1... | collective-permute-start | bytes 663560 | tf_op jit(solution)/shard_map/ppermute | solution.py:17
  27.2 1.9 collective-permute-start.1
  29.1 1.2 fusion.116
  30.3 0.4 fusion.117
  31.1 33.5 %collective-permute-done = f32[72,1,768]{2,0,1:T(8,128)S(1)} collective-permute-done((f32[72,1,768]{2,0,1:T(8,128)S(1)}, f32[72,1,768]{2,0,1:T(8,128)S(1)}, u32[]{:S(2)}, u32[]{:S(2)}) %collective-permute-start) | collective-permute-done | bytes 221216 | tf_op jit(solution)/shard_map/ppermute | solution.py:17
  64.6 9.3 %collective-permute-done.1 = f32[72,1,768]{2,0,1:T(8,128)S(1)} collective-permute-done((f32[72,1,768]{2,0,1:T(8,128)S(1)}, f32[72,1,768]{2,0,1:T(8,128)S(1)}, u32[]{:S(2)}, u32[]{:S(2)}) %collective-permute-start.1) | collective-permute-done | bytes 221216 | tf_op jit(solution)/shard_map/ppermute | solution.py:15
  73.9 0.6 fusion.47
  74.5 0.4 fusion.114
  75.0 16.0 %collective-permute-start.2 = (f32[72,1,768]{2,0,1:T(8,128)S(1)}, f32[72,1,768]{2,0,1:T(8,128)S(1)}, u32[]{:S(2)}, u32[]{:S(2)}) collective-permute-start(f32[72,1,768]{2,0,1:T(8,128)S(1)} %get-tuple-element.21), channel_id=1, source_target_pairs={{1,0},{2,1},{3,2},{4,3},{5,4},{6,5},{7,6},{8,7},{9,8},{10,9},{11,1... | collective-permute-start | bytes 663560 | tf_op jit(solution)/shard_map/ppermute | solution.py:17
  91.0 1.9 collective-permute-start.3
  93.1 18.0 %collective-permute-done.2 = f32[72,1,768]{2,0,1:T(8,128)S(1)} collective-permute-done((f32[72,1,768]{2,0,1:T(8,128)S(1)}, f32[72,1,768]{2,0,1:T(8,128)S(1)}, u32[]{:S(2)}, u32[]{:S(2)}) %collective-permute-start.2) | collective-permute-done | bytes 221216 | tf_op jit(solution)/shard_map/ppermute | solution.py:17
  111.0 12.3 %collective-permute-done.3 = f32[72,1,768]{2,0,1:T(8,128)S(1)} collective-permute-done((f32[72,1,768]{2,0,1:T(8,128)S(1)}, f32[72,1,768]{2,0,1:T(8,128)S(1)}, u32[]{:S(2)}, u32[]{:S(2)}) %collective-permute-start.3) | collective-permute-done | bytes 221216 | tf_op jit(solution)/shard_map/ppermute | solution.py:15
  123.4 0.6 fusion.42
  124.0 1.9 collective-permute-start.4
  126.0 27.4 %collective-permute-done.4 = f32[72,6,768]{2,0,1:T(8,128)} collective-permute-done((f32[72,6,768]{2,0,1:T(8,128)S(1)}, f32[72,6,768]{2,0,1:T(8,128)}, u32[]{:S(2)}, u32[]{:S(2)}) %collective-permute-start.4) | collective-permute-done | bytes 1327136 | tf_op jit(solution)/shard_map/ppermute | solution.py:27
  153.4 1.6 select_subtract_fusion
  155.0 0.4 copy.19
  155.6 10.4 %fusion.8 = f32[64,8,432]{2,1,0:T(8,128)} fusion(f32[432,768,1]{1,0,2:T(8,128)S(1)} %reshape.190, f32[64,8]{1,0:T(8,128)S(1)} %fusion.95, s32[64,8]{1,0:T(8,128)S(1)} %add_select_fusion.3, pred[64,8]{1,0:T(8,128)(4,1)S(1)} %fusion.94), kind=kOutput, calls=%fused_computation.12 | convolution fusion | flops 2042757120 | bytes 2216448 | tf_op jit(solution)/shard_map/kx,mx->km/dot_general | solution.py:120
  166.0 14.6 %all-to-all-start = ((f32[64,8,432]{2,1,0:T(8,128)}), f32[64,8,432]{2,1,0:T(8,128)S(1)}, u32[]{:S(2)}, u32[]{:S(2)}) async-start(f32[64,8,432]{2,1,0:T(8,128)} %fusion.8), calls=%async_computation | async-start | bytes 2097152 | tf_op jit(solution)/shard_map/all_to_all | solution.py:121
  180.6 64.4 %all-to-all-done = f32[64,8,432]{2,1,0:T(8,128)S(1)} async-done(((f32[64,8,432]{2,1,0:T(8,128)}), f32[64,8,432]{2,1,0:T(8,128)S(1)}, u32[]{:S(2)}, u32[]{:S(2)}) %all-to-all-start) | async-done | bytes 884768 | tf_op jit(solution)/shard_map/all_to_all | solution.py:121
  245.1 1.0 copy.20
  246.0 4.4 fusion.54
  250.5 4.8 convolution_bitcast_fusion
  255.3 0.9 copy.22
  256.2 2.0 copy.23
  258.1 7.1 %all-to-all-start.1 = ((f32[8,64,432]{2,0,1:T(8,128)}), f32[8,64,432]{2,0,1:T(8,128)S(1)}, u32[]{:S(2)}, u32[]{:S(2)}) async-start(f32[8,64,432]{2,0,1:T(8,128)} %copy.23), calls=%async_computation.1 | async-start | bytes 2097152 | tf_op jit(solution)/shard_map/all_to_all | solution.py:127
  265.3 45.4 %all-to-all-done.1 = f32[8,64,432]{2,0,1:T(8,128)S(1)} async-done(((f32[8,64,432]{2,0,1:T(8,128)}), f32[8,64,432]{2,0,1:T(8,128)S(1)}, u32[]{:S(2)}, u32[]{:S(2)}) %all-to-all-start.1) | async-done | bytes 884768 | tf_op jit(solution)/shard_map/all_to_all | solution.py:127
  310.7 0.3 copy.24
  311.2 10.1 %fusion.6 = f32[72,6,768]{2,0,1:T(8,128)} fusion(f32[72,6,512]{2,1,0:T(8,128)S(1)} %dot_general.20, f32[512]{0:T(512)S(1)} %fusion.97, s32[512]{0:T(512)S(1)} %add_select_fusion.4, pred[512]{0:T(512)(128)(4,1)S(1)} %iota_compare_fusion.2), kind=kOutput, calls=%fused_computation.10 | convolution fusion | flops 2042757120 | bytes 2216448 | tf_op jit(solution)/shard_map/kx,km->mx/dot_general | solution.py:85
  321.3 106.4 %collective-permute-start.5 = (f32[72,6,768]{2,0,1:T(8,128)}, f32[72,6,768]{2,0,1:T(8,128)}, u32[]{:S(2)}, u32[]{:S(2)}) collective-permute-start(f32[72,6,768]{2,0,1:T(8,128)} %fusion.6), channel_id=1, source_target_pairs={{64,0},{128,64},{192,128},{256,192},{320,256},{384,320},{448,384},... | collective-permute-start | bytes 3981320 | tf_op jit(solution)/shard_map/ppermute | solution.py:27
  428.4 0.4 copy.26
  429.1 3.1 gather_fusion
  432.3 3.6 scatter_custom_fusion
  436.1 85.8 %collective-permute-done.5 = f32[72,6,768]{2,0,1:T(8,128)} collective-permute-done((f32[72,6,768]{2,0,1:T(8,128)}, f32[72,6,768]{2,0,1:T(8,128)}, u32[]{:S(2)}, u32[]{:S(2)}) %collective-permute-start.5) | collective-permute-done | bytes 1327136 | tf_op jit(solution)/shard_map/ppermute | solution.py:27
  521.9 1.8 broadcast_multiply_fusion.1
  524.0 1.9 collective-permute-start.6
  525.9 2.4 collective-permute-start.7
  528.3 0.4 slice.158
  528.9 5.2 collective-permute-done.6
  534.1 25.3 %collective-permute-done.7 = f32[72,1,768]{2,0,1:T(8,128)S(1)} collective-permute-done((f32[72,1,768]{2,0,1:T(8,128)S(1)}, f32[72,1,768]{2,0,1:T(8,128)S(1)}, u32[]{:S(2)}, u32[]{:S(2)}) %collective-permute-start.7) | collective-permute-done | bytes 221216 | tf_op jit(solution)/shard_map/ppermute | solution.py:15
  559.4 0.6 broadcast_multiply_fusion
  560.2 1.9 collective-permute-start.8
  562.2 2.4 collective-permute-start.9
  564.6 0.4 slice.164
  565.1 1.9 collective-permute-done.8
  567.0 25.2 %collective-permute-done.9 = f32[72,1,768]{2,0,1:T(8,128)S(1)} collective-permute-done((f32[72,1,768]{2,0,1:T(8,128)S(1)}, f32[72,1,768]{2,0,1:T(8,128)S(1)}, u32[]{:S(2)}, u32[]{:S(2)}) %collective-permute-start.9) | collective-permute-done | bytes 221216 | tf_op jit(solution)/shard_map/ppermute | solution.py:15
  592.2 3.0 fusion.32
  (48 shorter events, 2.1 us)
Async XLA Ops:
  0.0 30.3 %copy-start = (f32[1,72,6,768]{3,1,2,0:T(8,128)S(1)}, f32[1,72,6,768]{3,1,2,0:T(8,128)}, u32[]{:S(2)}) copy-start(f32[1,72,6,768]{3,1,2,0:T(8,128)} %param.10) | copy-start | bytes 3981316
  1.2 63.4 %collective-permute-start = (f32[72,1,768]{2,0,1:T(8,128)S(1)}, f32[72,1,768]{2,0,1:T(8,128)S(1)}, u32[]{:S(2)}, u32[]{:S(2)}) collective-permute-start(f32[72,1,768]{2,0,1:T(8,128)S(1)} %get-tuple-element.27), channel_id=1, source_target_pairs={{1,0},{2,1},{3,2},{4,3},{5,4},{6,5},{7,6},{8,7},{9,8},{10,9},{11,1... | collective-permute-start | bytes 663560 | tf_op jit(solution)/shard_map/ppermute | solution.py:17
  27.2 46.7 %collective-permute-start.1 = (f32[72,1,768]{2,0,1:T(8,128)S(1)}, f32[72,1,768]{2,0,1:T(8,128)S(1)}, u32[]{:S(2)}, u32[]{:S(2)}) collective-permute-start(f32[72,1,768]{2,0,1:T(8,128)S(1)} %get-tuple-element.28), channel_id=1, source_target_pairs={{0,1},{1,2},{2,3},{3,4},{4,5},{5,6},{6,7},{7,8},{8,9},{9,10},{10,1... | collective-permute-start | bytes 663560 | tf_op jit(solution)/shard_map/ppermute | solution.py:15
  30.3 0.7 copy-start.3
  30.3 0.7 copy-start.4
  30.3 0.7 copy-start.5
  75.0 36.1 %collective-permute-start.2 = (f32[72,1,768]{2,0,1:T(8,128)S(1)}, f32[72,1,768]{2,0,1:T(8,128)S(1)}, u32[]{:S(2)}, u32[]{:S(2)}) collective-permute-start(f32[72,1,768]{2,0,1:T(8,128)S(1)} %get-tuple-element.21), channel_id=1, source_target_pairs={{1,0},{2,1},{3,2},{4,3},{5,4},{6,5},{7,6},{8,7},{9,8},{10,9},{11,1... | collective-permute-start | bytes 663560 | tf_op jit(solution)/shard_map/ppermute | solution.py:17
  91.0 32.4 %collective-permute-start.3 = (f32[72,1,768]{2,0,1:T(8,128)S(1)}, f32[72,1,768]{2,0,1:T(8,128)S(1)}, u32[]{:S(2)}, u32[]{:S(2)}) collective-permute-start(f32[72,1,768]{2,0,1:T(8,128)S(1)} %get-tuple-element.22), channel_id=1, source_target_pairs={{0,1},{1,2},{2,3},{3,4},{4,5},{5,6},{6,7},{7,8},{8,9},{9,10},{10,1... | collective-permute-start | bytes 663560 | tf_op jit(solution)/shard_map/ppermute | solution.py:15
  124.0 29.4 %copy-start.1 = (f32[72,6,768]{2,0,1:T(8,128)}, f32[72,6,768]{2,0,1:T(8,128)S(1)}, u32[]{:S(2)}) copy-start(f32[72,6,768]{2,0,1:T(8,128)S(1)} %fusion.42) | copy-start | bytes 3981316
  124.0 29.4 %collective-permute-start.4 = (f32[72,6,768]{2,0,1:T(8,128)S(1)}, f32[72,6,768]{2,0,1:T(8,128)}, u32[]{:S(2)}, u32[]{:S(2)}) collective-permute-start(f32[72,6,768]{2,0,1:T(8,128)S(1)} %fusion.42), channel_id=1, source_target_pairs={{0,64},{64,128},{128,192},{192,256},{256,320},{320,384},{384,448},... | collective-permute-start | bytes 3981320 | tf_op jit(solution)/shard_map/ppermute | solution.py:27
  166.0 79.1 %all-to-all-start = ((f32[64,8,432]{2,1,0:T(8,128)}), f32[64,8,432]{2,1,0:T(8,128)S(1)}, u32[]{:S(2)}, u32[]{:S(2)}) async-start(f32[64,8,432]{2,1,0:T(8,128)} %fusion.8), calls=%async_computation | async-start | bytes 2097152 | tf_op jit(solution)/shard_map/all_to_all | solution.py:121
  245.1 1.0 copy-start.9
  258.1 52.6 %all-to-all-start.1 = ((f32[8,64,432]{2,0,1:T(8,128)}), f32[8,64,432]{2,0,1:T(8,128)S(1)}, u32[]{:S(2)}, u32[]{:S(2)}) async-start(f32[8,64,432]{2,0,1:T(8,128)} %copy.23), calls=%async_computation.1 | async-start | bytes 2097152 | tf_op jit(solution)/shard_map/all_to_all | solution.py:127
  311.2 117.2 %copy-start.8 = (s32[1,512]{1,0:T(1,128)S(1)}, s32[1,512]{1,0:T(1,128)}, u32[]{:S(2)}) copy-start(s32[1,512]{1,0:T(1,128)} %param.16) | copy-start | bytes 6148
  311.2 117.2 %copy-start.2 = (f32[72,6,768]{2,0,1:T(8,128)S(1)}, f32[72,6,768]{2,0,1:T(8,128)}, u32[]{:S(2)}) copy-start(f32[72,6,768]{2,0,1:T(8,128)} %copy-done.1) | copy-start | bytes 3981316
  321.3 200.6 %collective-permute-start.5 = (f32[72,6,768]{2,0,1:T(8,128)}, f32[72,6,768]{2,0,1:T(8,128)}, u32[]{:S(2)}, u32[]{:S(2)}) collective-permute-start(f32[72,6,768]{2,0,1:T(8,128)} %fusion.6), channel_id=1, source_target_pairs={{64,0},{128,64},{192,128},{256,192},{320,256},{384,320},{448,384},... | collective-permute-start | bytes 3981320 | tf_op jit(solution)/shard_map/ppermute | solution.py:27
  429.1 3.2 copy-start.6
  429.1 3.2 copy-start.7
  524.0 10.1 %collective-permute-start.6 = (f32[72,1,768]{2,0,1:T(8,128)S(1)}, f32[72,1,768]{2,0,1:T(8,128)S(1)}, u32[]{:S(2)}, u32[]{:S(2)}) collective-permute-start(f32[72,1,768]{2,0,1:T(8,128)S(1)} %get-tuple-element.13), channel_id=1, source_target_pairs={{1,0},{2,1},{3,2},{4,3},{5,4},{6,5},{7,6},{8,7},{9,8},{10,9},{11,1... | collective-permute-start | bytes 663560 | tf_op jit(solution)/shard_map/ppermute | solution.py:17
  525.9 33.5 %collective-permute-start.7 = (f32[72,1,768]{2,0,1:T(8,128)S(1)}, f32[72,1,768]{2,0,1:T(8,128)S(1)}, u32[]{:S(2)}, u32[]{:S(2)}) collective-permute-start(f32[72,1,768]{2,0,1:T(8,128)S(1)} %get-tuple-element.14), channel_id=1, source_target_pairs={{0,1},{1,2},{2,3},{3,4},{4,5},{5,6},{6,7},{7,8},{8,9},{9,10},{10,1... | collective-permute-start | bytes 663560 | tf_op jit(solution)/shard_map/ppermute | solution.py:15
  560.2 6.8 %collective-permute-start.8 = (f32[72,1,768]{2,0,1:T(8,128)S(1)}, f32[72,1,768]{2,0,1:T(8,128)S(1)}, u32[]{:S(2)}, u32[]{:S(2)}) collective-permute-start(f32[72,1,768]{2,0,1:T(8,128)S(1)} %get-tuple-element.11), channel_id=1, source_target_pairs={{1,0},{2,1},{3,2},{4,3},{5,4},{6,5},{7,6},{8,7},{9,8},{10,9},{11,1... | collective-permute-start | bytes 663560 | tf_op jit(solution)/shard_map/ppermute | solution.py:17
  562.2 30.0 %collective-permute-start.9 = (f32[72,1,768]{2,0,1:T(8,128)S(1)}, f32[72,1,768]{2,0,1:T(8,128)S(1)}, u32[]{:S(2)}, u32[]{:S(2)}) collective-permute-start(f32[72,1,768]{2,0,1:T(8,128)S(1)} %get-tuple-element.12), channel_id=1, source_target_pairs={{0,1},{1,2},{2,3},{3,4},{4,5},{5,6},{6,7},{7,8},{8,9},{9,10},{10,1... | collective-permute-start | bytes 663560 | tf_op jit(solution)/shard_map/ppermute | solution.py:15
where the time goes:
time: 603 us; the launch traced here: 596 us
  waiting for transfers between devices  354 us (59%)
  starting transfers between devices  185 us (31%)
  matrix products  29.7 us (5%)
  local copies, waits for them, and re-layouts  13.7 us (2%)
  other arithmetic  12.4 us (2%)
    ppermute x2, waiting for transfers between devices, passed_along(): return lax.ppermute(block, axis, route)  113 us
    ppermute x2, starting transfers between devices, passed_along(): return lax.ppermute(block, axis, route)  108 us
    ppermute x4, waiting for transfers between devices, with_halo(): lax.ppermute(tail, axis, [(i, (i + 1) % count) for i in range(ends)])  72 us
    all_to_all x1, waiting for transfers between devices, body(): lax.all_to_all(coefs, 'tile', split_axis=0, concat_axis=1, tiled=True)  64.4 us
    ppermute x4, waiting for transfers between devices, with_halo(): lax.ppermute(head, axis, [((i + 1) % count, i) for i in range(ends)])  58.5 us
    ppermute x4, starting transfers between devices, with_halo(): lax.ppermute(head, axis, [((i + 1) % count, i) for i in range(ends)])  45.9 us
    all_to_all x1, waiting for transfers between devices, body(): lax.all_to_all(back, 'tile', split_axis=1, concat_axis=0, tiled=True)  45.4 us
    all_to_all x1, starting transfers between devices, body(): lax.all_to_all(coefs, 'tile', split_axis=0, concat_axis=1, tiled=True)  14.6 us
  transfers between devices with their start and end apart: 12, of which 12 were waited for; matrix products, arithmetic and copies ran while one was open for 2% of the time, Pallas kernels for 0%

commit v1 on v0

v1 whole, which is shorter than its diff:
```python
import jax
import jax.numpy as jnp
import ml_dtypes
import numpy as np
from jax import lax
from jax.experimental import pallas as pl
from jax.experimental.pallas import tpu as pltpu
from jax.sharding import PartitionSpec as P

LEV, LON, ROWS, KEEP, NLAT, TILES, NWIN = 72, 768, 6, 512, 384, 64, 16
EXT = 8
PLANE = LEV * LON
UNITS = 5
VMEM_LIMIT = 40 * 1024 * 1024


def zonal_table():
    half = KEEP // 2
    wave = np.arange(KEEP)
    number = np.where(wave < half, wave, wave - half + 1)
    phase = number[:, None] * np.arange(LON)[None, :] % LON
    angle = 2.0 * np.pi * phase / LON
    scale = np.where(wave == 0, np.sqrt(1.0 / LON), np.sqrt(2.0 / LON))
    return np.where((wave < half)[:, None], np.cos(angle), np.sin(angle)) * scale[:, None]


def meridional_table():
    modes = np.arange(NLAT)
    phase = modes[:, None] * (2 * modes[None, :] + 1) % (4 * NLAT)
    scale = np.where(modes == 0, np.sqrt(1.0 / NLAT), np.sqrt(2.0 / NLAT))
    return np.cos(np.pi * phase / (2.0 * NLAT)) * scale[:, None]


def extended_meridional():
    table = meridional_table()
    out = np.zeros((NLAT, TILES, EXT))
    for tile in range(TILES):
        for i in range(EXT):
            row = tile * ROWS + (i if tile % 2 else ROWS - 1 - i)
            if 0 <= row < NLAT:
                out[:, tile, i] = table[:, row]
    return out.reshape(NLAT, TILES * EXT)


def two_parts(table):
    high = table.astype(ml_dtypes.bfloat16)
    low = (table - high.astype(np.float64)).astype(ml_dtypes.bfloat16)
    return high, low


def split(x):
    high = x.astype(jnp.bfloat16)
    low = (x - high.astype(jnp.float32)).astype(jnp.bfloat16)
    return high, low


def dot(a, b):
    return jnp.dot(a, b, preferred_element_type=jnp.float32)


def dot3(a, b):
    return dot(a[0], b[0]) + (dot(a[0], b[1]) + dot(a[1], b[0]))


def source_row(core, i):
    return jnp.where(core == 0, ROWS - 1 - i, i)


def project_kernel(flags, inc, bg, zh, zl, out):
    core = flags[0]
    first = (flags[1] == 0).astype(jnp.float32)
    field = inc[...] - first * bg[...]
    coefs = dot3(split(field.reshape(ROWS * LEV, LON)), (zh[...], zl[...]))
    coefs = coefs.reshape(ROWS, LEV, KEEP)
    for i in range(ROWS):
        out[source_row(core, i)] = coefs[i]


def coef_rows(core, lat, lon, drift, inner, outer):
    def pick(own, near, far):
        def get(r):
            if r < 0:
                return inner[near[-1 - r], :][None, :]
            if r >= ROWS:
                return outer[far[r - ROWS], :][None, :]
            return own[pl.ds(source_row(core, r), 1), :]

        return get

    return pick(lat, (0, 1), (0, 1)), pick(lon, (2,), (2,)), pick(drift, (3,), (3,))


def weights(a, b, c):
    return 1.0 - 2.0 * a - 2.0 * b, b - 0.5 * c, b + 0.5 * c


def forward_kernel(flags, inc, near, lat, lon, drift, inner, outer, zh, zl, p_out, y_out, mid):
    core = flags[0]
    la, lo, dr = coef_rows(core, lat, lon, drift, inner, outer)

    def state(r):
        if r < 0:
            return near[-1 - r]
        return inc[source_row(core, r)]

    def step(get, r, lowest, highest):
        a = la(r)
        if r > highest:
            return a * get(r - 1)
        cen, east, west = weights(a, lo(r), dr(r))
        mine = get(r)
        beside = get(r - 1)
        if r < highest:
            beside = beside + get(r + 1)
        return (
            cen * mine
            + a * beside
            + east * pltpu.roll(mine, LON - 1, 1)
            + west * pltpu.roll(mine, 1, 1)
        )

    for r in range(-1, ROWS + 1):
        mid[r + 1] = step(state, r, -2, ROWS - 1)
    for r in range(EXT):
        p_out[r] = step(lambda q: mid[q + 1], r, -1, ROWS)
    y = dot3(split(p_out[...].reshape(EXT * LEV, LON)), (zh[...], zl[...]))
    y_out[...] = y.reshape(EXT, LEV, KEEP)


def unit_base(i, quarter, block):
    return quarter * 640 + (block % 2) * 40 + (block // 2) * 8 + i


def arrange_kernel(flags, shifted, y, out):
    keep = (flags[1] != NWIN - 1).astype(jnp.float32)
    for quarter in range(4):
        for slot in range(8):
            base = quarter * 640 + slot * 80 + 40 + 32
            out[base : base + 8, :] = jnp.zeros((8, 128), jnp.float32)
    for i in range(EXT):
        coefs = -keep * y[i]
        if i < ROWS:
            coefs = shifted[i] + coefs
        for quarter in range(4):
            for block in range(9):
                out[pl.ds(unit_base(i, quarter, block), 8, stride=80), :] = coefs[
                    block * 8 : block * 8 + 8, quarter * 128 : quarter * 128 + 128
                ]


def modal_kernel(got, spec, ph, pl_, qh, ql, out):
    data = got[...].reshape(TILES, UNITS, EXT, 128)
    x = jnp.concatenate([data[:, u].reshape(TILES * EXT, 128) for u in range(UNITS)], axis=1)
    modal = dot3((ph[...], pl_[...]), split(x))
    scale = spec[...].T
    modal = modal * jnp.concatenate([scale] * UNITS, axis=1)
    back = dot3((qh[...], ql[...]), split(modal))
    for u in range(UNITS):
        out[:, u * 8 : u * 8 + 8, :] = back[:, u * 128 : u * 128 + 128].reshape(TILES, EXT, 128)


def collect_kernel(got, own, far):
    for i in range(EXT):
        for quarter in range(4):
            for block in range(9):
                tile = got[pl.ds(unit_base(i, quarter, block), 8, stride=80), :]
                rows = pl.ds(block * 8, 8)
                lanes = pl.ds(quarter * 128, 128)
                if i < ROWS:
                    own[i, rows, lanes] = tile
                else:
                    far[i - ROWS, rows, lanes] = tile


def forcing_kernel(flags, own, far, placed, zh, zl, out):
    keep = (flags[1] != NWIN - 1).astype(jnp.float32)
    table = (zh[...], zl[...])
    field = dot3(split(own[...].reshape(ROWS * LEV, KEEP)), table).reshape(ROWS, LEV, LON)
    out[:ROWS] = keep * field - placed[:ROWS]
    field = dot3(split(far[...].reshape(2 * LEV, KEEP)), table).reshape(2, LEV, LON)
    out[ROWS:] = keep * field - placed[ROWS:]


def adjoint_kernel(flags, force, near, lat, lon, drift, inner, outer, out, mid):
    core = flags[0]
    la, lo, dr = coef_rows(core, lat, lon, drift, inner, outer)

    def start(r):
        if r < 0:
            return near[-1 - r]
        return force[r]

    def step(get, r):
        cen, east, west = weights(la(r), lo(r), dr(r))
        mine = get(r)
        return (
            cen * mine
            + la(r + 1) * get(r + 1)
            + la(r - 1) * get(r - 1)
            + pltpu.roll(east * mine, 1, 1)
            + pltpu.roll(west * mine, LON - 1, 1)
        )

    for r in range(-1, ROWS + 1):
        mid[r + 1] = step(start, r)
    for r in range(ROWS):
        out[r] = step(lambda q: mid[q + 1], r)


def finish_kernel(flags, shifted, adjoint, zh, zl, out):
    core = flags[0]
    field = dot3(split(shifted[...].reshape(ROWS * LEV, KEEP)), (zh[...], zl[...]))
    field = field.reshape(ROWS, LEV, LON)
    for i in range(ROWS):
        out[source_row(core, i)] = field[i] - adjoint[i]


def call(kernel, shapes, args, scratch=(), scalar=True, cost=None):
    specs = [pl.BlockSpec(memory_space=pltpu.VMEM)] * len(args)
    if scalar:
        specs[0] = pl.BlockSpec(memory_space=pltpu.SMEM)
    shapes = [jax.ShapeDtypeStruct(s, jnp.float32) for s in shapes]
    single = len(shapes) == 1
    return pl.pallas_call(
        kernel,
        out_shape=shapes[0] if single else shapes,
        in_specs=specs,
        out_specs=(
            pl.BlockSpec(memory_space=pltpu.VMEM)
            if single
            else [pl.BlockSpec(memory_space=pltpu.VMEM)] * len(shapes)
        ),
        scratch_shapes=[pltpu.VMEM(s, jnp.float32) for s in scratch],
        compiler_params=pltpu.CompilerParams(vmem_limit_bytes=VMEM_LIMIT),
        cost_estimate=pl.CostEstimate(
            flops=cost or 10_000_000, bytes_accessed=4_000_000, transcendentals=0
        ),
    )(*args)


def body(
    increment,
    background,
    lat_diffusion,
    lon_diffusion,
    advection,
    spectrum,
    obs_index,
    obs_count,
    innovation,
    obs_precision,
):
    tile = lax.axis_index("tile")
    core = tile % 2
    window = lax.axis_index("win")
    flags = jnp.stack([core, window]).astype(jnp.int32)
    inner_pairs = [(t, t ^ 1) for t in range(TILES)]
    outer_pairs = [(t, t + 1 if t % 2 else t - 1) for t in range(1, TILES - 1)]
    earlier = [(w, (w - 1) % NWIN) for w in range(NWIN)]
    later = [(w, (w + 1) % NWIN) for w in range(NWIN)]

    zonal = zonal_table()
    zonal_back = two_parts(zonal)
    zonal_fwd = tuple(np.ascontiguousarray(part.T) for part in zonal_back)
    merid = extended_meridional()
    merid_fwd = two_parts(merid)
    merid_back = tuple(np.ascontiguousarray(part.T) for part in merid_fwd)

    inc = increment[0].transpose(1, 0, 2)
    bg = background.transpose(1, 0, 2)
    lat, lon, drift = lat_diffusion[0], lon_diffusion[0], advection[0]

    def in_order(rows):
        return jnp.where(core == 0, rows[::-1], rows)

    coefs = call(project_kernel, [(ROWS, LEV, KEEP)], (flags, inc, bg, *zonal_fwd), cost=10**9)
    shifted = lax.ppermute(coefs, "win", earlier)

    near = lax.ppermute(jnp.where(core == 0, inc[:3:-1], inc[:2]), "tile", inner_pairs)
    lat_o, lon_o, drift_o = in_order(lat), in_order(lon), in_order(drift)
    inner = lax.ppermute(
        jnp.stack([lat_o[0], lat_o[1], lon_o[0], drift_o[0]]), "tile", inner_pairs
    )
    cells = obs_index[0]
    live = jnp.arange(cells.shape[0], dtype=jnp.int32) < obs_count[0, 0]
    rest = cells % (ROWS * LON)
    row = rest // LON
    place = jnp.where(core == 0, ROWS - 1 - row, row)
    own_at = (place * LEV + cells // (ROWS * LON)) * LON + rest % LON
    sent = jnp.where(live, own_at, 0).astype(jnp.float32)
    outer = lax.ppermute(
        jnp.concatenate([lat_o[5], lat_o[4], lon_o[5], drift_o[5], sent]), "tile", outer_pairs
    )
    far_cells = outer[4 * LON :].astype(jnp.int32)
    outer = outer[: 4 * LON].reshape(4, LON)
    edge = far_cells >= 4 * PLANE
    far_at = (11 - far_cells // PLANE) * PLANE + far_cells % PLANE

    p, y = call(
        forward_kernel,
        [(EXT, LEV, LON), (EXT, LEV, KEEP)],
        (flags, inc, near, lat, lon, drift, inner, outer, *zonal_fwd),
        scratch=[(EXT, LEV, LON)],
        cost=10**9,
    )
    send = call(arrange_kernel, [(TILES * UNITS * EXT, 128)], (flags, shifted, y))
    send = send.reshape(TILES, UNITS * EXT, 128)
    groups = [list(range(g * 16, g * 16 + 16)) for g in range(4)]
    spec = lax.all_gather(spectrum, "tile", axis_index_groups=groups, tiled=True)
    got = lax.all_to_all(send, "tile", split_axis=0, concat_axis=0, tiled=True)

    found = p.reshape(-1)[jnp.concatenate([own_at, jnp.where(edge, far_at, 0)])]
    values = found[:512] + lax.ppermute(
        jnp.where(edge, found[512:], 0.0), "tile", outer_pairs
    )
    departure = jnp.where(
        live, obs_precision[0] * (values - innovation[0]), jnp.zeros_like(values)
    )
    far_departure = lax.ppermute(departure, "tile", outer_pairs)
    placed = (
        jnp.zeros((EXT * PLANE,), jnp.float32)
        .at[jnp.concatenate([own_at, jnp.where(edge, far_at, EXT * PLANE)])]
        .add(jnp.concatenate([departure, far_departure]), mode="drop")
        .reshape(EXT, LEV, LON)
    )

    back = call(
        modal_kernel,
        [(TILES, UNITS * EXT, 128)],
        (got, spec, *merid_fwd, *merid_back),
        scalar=False,
        cost=10**9,
    )
    grid = lax.all_to_all(back, "tile", split_axis=0, concat_axis=0, tiled=True)
    own, far = call(
        collect_kernel,
        [(ROWS, LEV, KEEP), (2, LEV, KEEP)],
        (grid.reshape(TILES * UNITS * EXT, 128),),
        scalar=False,
    )
    at_home = lax.ppermute(own, "win", later)
    force = call(
        forcing_kernel, [(EXT, LEV, LON)], (flags, own, far, placed, *zonal_back), cost=10**9
    )
    force_near = lax.ppermute(force[:2], "tile", inner_pairs)
    adjoint = call(
        adjoint_kernel,
        [(ROWS, LEV, LON)],
        (flags, force, force_near, lat, lon, drift, inner, outer),
        scratch=[(EXT, LEV, LON)],
    )
    gradient = call(
        finish_kernel, [(ROWS, LEV, LON)], (flags, at_home, adjoint, *zonal_back), cost=10**9
    )
    return gradient.transpose(1, 0, 2)[None]


def solution(mesh):
    in_specs = (
        P("win", None, "tile", None),
        P(None, "tile", None),
        P("win", "tile", None),
        P("win", "tile", None),
        P("win", "tile", None),
        P("tile", None),
        P("win", "tile"),
        P("win", "tile"),
        P("win", "tile"),
        P("win", "tile"),
    )
    out_specs = P("win", None, "tile", None)
    return jax.shard_map(body, mesh=mesh, in_specs=in_specs, out_specs=out_specs, check_vma=False)
```

time: 603 us -> 503 us (0.83)
  the two profiles are of different devices: /device:TPU:152 before, /device:TPU:1 now
where the time goes in v1:
time: 503 us; the launch traced here: 498 us
  starting transfers between devices  197 us (39%)
  blocking collectives  169 us (34%)
  waiting for transfers between devices  54 us (11%)
  local copies, waits for them, and re-layouts  45.6 us (9%)
  Pallas kernels  22.9 us (5%)
  other arithmetic  8.55 us (2%)
    all_gather x1, blocking collectives, body(): lax.all_gather(spectrum, 'tile', axis_index_groups=groups, tiled=True)  169 us
    ppermute x1, starting transfers between devices, body(): at_home = lax.ppermute(own, 'win', later)  106 us
    gather x1, local copies, waits for them, and re-layouts, body(): found = p.reshape(-1)[jnp.concatenate([own_at, jnp.where(edge, far_at, 0)])]  28.2 us
    pallas_call x8, Pallas kernels, call(): pl.pallas_call(kernel, out_shape=shapes[0] if single else shapes, in_spec...  22.9 us
    ppermute x1, waiting for transfers between devices, body(): lax.ppermute(jnp.where(edge, found[512:], 0.0), 'tile', outer_pairs)  21 us
    all_to_all x1, starting transfers between devices, body(): got = lax.all_to_all(send, 'tile', split_axis=0, concat_axis=0, tiled=True)  19.4 us
    ppermute x1, starting transfers between devices, body(): far_departure = lax.ppermute(departure, 'tile', outer_pairs)  18.6 us
    ppermute x1, waiting for transfers between devices, body(): lax.ppermute(jnp.concatenate([lat_o[5], lat_o[4], lon_o[5], drift_o[5], s...  16.1 us
  transfers between devices with their start and end apart: 10, of which 5 were waited for; matrix products, arithmetic and copies ran while one was open for 8% of the time, Pallas kernels for 2%

profile of v1, /device:TPU:1, one launch (start us, length us, event | category | flops | bytes accessed | tf_op | source)
XLA Modules:
  0.0 497.7 jit_solution(15195239521368184820)
XLA Ops:
  0.0 1.2 slice.60
  1.2 1.1 slice_select_fusion
  2.3 16.1 %collective-permute-start.1 = (f32[2,72,768]{2,1,0:T(8,128)S(1)}, f32[2,72,768]{2,1,0:T(8,128)S(1)}, u32[]{:S(2)}, u32[]{:S(2)}) collective-permute-start(f32[2,72,768]{2,1,0:T(8,128)S(1)} %slice_select_fusion), channel_id=1, source_target_pairs={{0,1},{1,0},{2,3},{3,2},{4,5},{5,4},{6,7},{7,6},{8,9},{9,8},{10,11... | collective-permute-start | bytes 1327112 | tf_op jit(solution)/shard_map/ppermute | solution.py:279
  18.4 0.1 pad_add_fusion.flags
  18.4 1.3 copy-done.3
  19.8 1.1 copy-done.6
  20.9 2.7 shard_map.172
  23.6 13.5 %collective-permute-start = (f32[6,72,512]{2,1,0:T(8,128)}, f32[6,72,512]{2,1,0:T(8,128)}, u32[]{:S(2)}, u32[]{:S(2)}) collective-permute-start(f32[6,72,512]{2,1,0:T(8,128)} %shard_map.172), channel_id=1, source_target_pairs={{0,960},{64,0},{128,64},{192,128},{256,192},{320,256},{384,320},{4... | collective-permute-start | bytes 2654216 | tf_op jit(solution)/shard_map/ppermute | solution.py:277
  37.2 0.2 rev.13
  37.4 0.2 rev.14
  37.6 0.2 rev.15
  38.6 11.7 %collective-permute-start.3 = (f32[3584]{0:T(1024)S(1)}, f32[3584]{0:T(1024)S(1)}, u32[]{:S(2)}, u32[]{:S(2)}) collective-permute-start(f32[3584]{0:T(1024)S(1)} %get-tuple-element.18), channel_id=1, source_target_pairs={{1,2},{2,1},{3,4},{4,3},{5,6},{6,5},{7,8},{8,7},{9,10},{10,9},{11,... | collective-permute-start | bytes 43016 | tf_op jit(solution)/shard_map/ppermute | solution.py:291
  50.4 1.9 collective-permute-start.2
  52.3 16.1 %collective-permute-done.3 = f32[3584]{0:T(1024)S(1)} collective-permute-done((f32[3584]{0:T(1024)S(1)}, f32[3584]{0:T(1024)S(1)}, u32[]{:S(2)}, u32[]{:S(2)}) %collective-permute-start.3) | collective-permute-done | bytes 14368 | tf_op jit(solution)/shard_map/ppermute | solution.py:291
  68.5 0.0 collective-permute-done.1.near
  68.5 0.8 copy-done.14
  69.3 1.1 copy-done.5
  70.4 1.1 copy-done.7
  71.5 1.0 copy-done.15
  72.5 3.6 shard_map.173
  76.1 2.7 shard_map.174
  78.8 19.4 %all-to-all-start = ((f32[64,40,128]{2,1,0:T(8,128)}), f32[64,40,128]{2,1,0:T(8,128)S(1)}, u32[]{:S(2)}, u32[]{:S(2)}) async-start(f32[64,40,128]{2,1,0:T(8,128)} %bitcast.9), calls=%async_computation | async-start | bytes 2621440 | tf_op jit(solution)/shard_map/all_to_all | solution.py:310
  98.3 169.0 %all_gather.3.spec = f32[128,384]{1,0:T(8,128)S(1)} all-gather(f32[8,384]{1,0:T(8,128)S(1)} %copy-done.19), channel_id=1, replica_groups={{0,1,2,3,4,5,6,7,8,9,10,11,12,13,14,15},{16,17,18,19,20,21,22,23,24,25,..., dimensions={0}, use_global_device_ids=true | all-gather | bytes 208896 | tf_op jit(solution)/shard_map/all_gather | solution.py:309
  267.3 1.0 copy-done.8
  268.3 1.0 copy-done.9
  269.3 1.0 copy-done.10
  270.3 1.0 copy-done.11
  271.3 3.8 shard_map.175
  275.1 5.6 %all-to-all-start.1 = ((f32[64,40,128]{2,1,0:T(8,128)}), f32[64,40,128]{2,1,0:T(8,128)S(1)}, u32[]{:S(2)}, u32[]{:S(2)}) async-start(f32[64,40,128]{2,1,0:T(8,128)} %shard_map.175), calls=%async_computation.1 | async-start | bytes 2621440 | tf_op jit(solution)/shard_map/all_to_all | solution.py:334
  280.7 1.4 reshape.176
  282.1 28.2 %gather_fusion = f32[1024]{0:T(1024)S(1)} fusion(f32[442368]{0:T(1024)} %reshape.176, s32[1024]{0:T(1024)S(1)} %broadcast_clamp_fusion), kind=kCustom, calls=%fused_computation | custom fusion | bytes 12288 | tf_op jit(solution)/shard_map/gather | solution.py:312
  310.4 10.4 %all-to-all-done.1 = f32[64,40,128]{2,1,0:T(8,128)S(1)} async-done(((f32[64,40,128]{2,1,0:T(8,128)}), f32[64,40,128]{2,1,0:T(8,128)S(1)}, u32[]{:S(2)}, u32[]{:S(2)}) %all-to-all-start.1) | async-done | bytes 1310752 | tf_op jit(solution)/shard_map/all_to_all | solution.py:334
  320.8 1.3 shard_map.176
  322.0 0.7 copy-done.12
  322.8 105.7 %collective-permute-start.4 = (f32[6,72,512]{2,1,0:T(8,128)}, f32[6,72,512]{2,1,0:T(8,128)}, u32[]{:S(2)}, u32[]{:S(2)}) collective-permute-start(f32[6,72,512]{2,1,0:T(8,128)} %get-tuple-element.10.own), channel_id=1, source_target_pairs={{0,64},{64,128},{128,192},{192,256},{256,320},{320,384},{384,448},... | collective-permute-start | bytes 2654216 | tf_op jit(solution)/shard_map/ppermute | solution.py:341
  428.5 2.2 collective-permute-start.5
  430.7 21.0 %collective-permute-done.5 = f32[512]{0:T(512)S(1)} collective-permute-done((f32[512]{0:T(512)S(1)}, f32[512]{0:T(512)S(1)}, u32[]{:S(2)}, u32[]{:S(2)}) %collective-permute-start.5) | collective-permute-done | bytes 2080 | tf_op jit(solution)/shard_map/ppermute | solution.py:313
  451.7 18.6 %collective-permute-start.6 = (f32[512]{0:T(512)S(1)}, f32[512]{0:T(512)S(1)}, u32[]{:S(2)}, u32[]{:S(2)}) collective-permute-start(f32[512]{0:T(512)S(1)} %multiply_select_fusion), channel_id=1, source_target_pairs={{1,2},{2,1},{3,4},{4,3},{5,6},{6,5},{7,8},{8,7},{9,10},{10,9},{11,... | collective-permute-start | bytes 6152 | tf_op jit(solution)/shard_map/ppermute | solution.py:319
  470.3 4.7 collective-permute-done.6
  475.0 7.2 %scatter_custom_fusion = f32[442368]{0:T(1024)} fusion(s32[1024]{0:T(1024)S(1)} %bitcast.59, f32[1024]{0:T(1024)S(1)} %pad_maximum_fusion.1, f32[]{:T(128)} %constant.94.clone.1), kind=kCustom, calls=%fused_computation.2 | custom fusion | flops 1024 | bytes 1769476 | tf_op jit(solution)/shard_map/scatter-add | solution.py:323
  482.2 1.7 reshape.177.placed
  484.0 0.1 copy-done.2
  484.1 1.0 copy-done.13
  485.1 2.7 shard_map.177.force
  487.9 1.9 collective-permute-start.7
  489.8 1.8 collective-permute-done.7.near
  491.5 2.6 shard_map.178.adjoint
  494.2 3.5 shard_map.179
  (65 shorter events, 0.4 us)
Async XLA Ops:
  0.0 18.4 %copy-start.4 = (bf16[768,512]{1,0:T(8,128)(2,1)S(1)}, bf16[768,512]{1,0:T(8,128)(2,1)}, u32[]{:S(2)}) copy-start(bf16[768,512]{1,0:T(8,128)(2,1)} %constant.100.clone.zl) | copy-start | bytes 2359300
  0.0 18.4 %copy-start = (f32[1,72,6,768]{3,1,2,0:T(8,128)S(1)}, f32[1,72,6,768]{3,1,2,0:T(8,128)}, u32[]{:S(2)}) copy-start(f32[1,72,6,768]{3,1,2,0:T(8,128)} %param.18) | copy-start | bytes 3981316
  2.3 66.2 %collective-permute-start.1 = (f32[2,72,768]{2,1,0:T(8,128)S(1)}, f32[2,72,768]{2,1,0:T(8,128)S(1)}, u32[]{:S(2)}, u32[]{:S(2)}) collective-permute-start(f32[2,72,768]{2,1,0:T(8,128)S(1)} %slice_select_fusion), channel_id=1, source_target_pairs={{0,1},{1,0},{2,3},{3,2},{4,5},{5,4},{6,7},{7,6},{8,9},{9,8},{10,11... | collective-permute-start | bytes 1327112 | tf_op jit(solution)/shard_map/ppermute | solution.py:279
  18.4 1.3 copy-start.3
  19.8 1.1 copy-start.6
  20.9 16.2 %copy-start.20 = (s32[1,512]{1,0:T(1,128)S(1)}, s32[1,512]{1,0:T(1,128)}, u32[]{:S(2)}) copy-start(s32[1,512]{1,0:T(1,128)} %param.24) | copy-start | bytes 6148
  20.9 16.3 %copy-start.16 = (f32[1,6,768]{2,0,1:T(1,128)S(1)}, f32[1,6,768]{2,0,1:T(1,128)}, u32[]{:S(2)}) copy-start(f32[1,6,768]{2,0,1:T(1,128)} %param.20) | copy-start | bytes 55300
  20.9 16.5 %copy-start.17 = (f32[1,6,768]{2,0,1:T(1,128)S(1)}, f32[1,6,768]{2,0,1:T(1,128)}, u32[]{:S(2)}) copy-start(f32[1,6,768]{2,0,1:T(1,128)} %param.21) | copy-start | bytes 55300
  20.9 16.7 %copy-start.18 = (f32[1,6,768]{2,0,1:T(1,128)S(1)}, f32[1,6,768]{2,0,1:T(1,128)}, u32[]{:S(2)}) copy-start(f32[1,6,768]{2,0,1:T(1,128)} %param.22) | copy-start | bytes 55300
  23.6 52.5 %collective-permute-start = (f32[6,72,512]{2,1,0:T(8,128)}, f32[6,72,512]{2,1,0:T(8,128)}, u32[]{:S(2)}, u32[]{:S(2)}) collective-permute-start(f32[6,72,512]{2,1,0:T(8,128)} %shard_map.172), channel_id=1, source_target_pairs={{0,960},{64,0},{128,64},{192,128},{256,192},{320,256},{384,320},{4... | collective-permute-start | bytes 2654216 | tf_op jit(solution)/shard_map/ppermute | solution.py:277
  38.6 29.8 %collective-permute-start.3 = (f32[3584]{0:T(1024)S(1)}, f32[3584]{0:T(1024)S(1)}, u32[]{:S(2)}, u32[]{:S(2)}) collective-permute-start(f32[3584]{0:T(1024)S(1)} %get-tuple-element.18), channel_id=1, source_target_pairs={{1,2},{2,1},{3,4},{4,3},{5,6},{6,5},{7,8},{8,7},{9,10},{10,9},{11,... | collective-permute-start | bytes 43016 | tf_op jit(solution)/shard_map/ppermute | solution.py:291
  50.4 18.1 %collective-permute-start.2 = (f32[4,768]{1,0:T(4,128)S(1)}, f32[4,768]{1,0:T(4,128)S(1)}, u32[]{:S(2)}, u32[]{:S(2)}) collective-permute-start(f32[4,768]{1,0:T(4,128)S(1)} %pad_maximum_fusion), channel_id=1, source_target_pairs={{0,1},{1,0},{2,3},{3,2},{4,5},{5,4},{6,7},{7,6},{8,9},{9,8},{10,11... | collective-permute-start | bytes 36872 | tf_op jit(solution)/shard_map/ppermute | solution.py:281
  68.5 0.8 copy-start.14
  69.3 1.1 copy-start.5
  70.4 1.1 copy-start.7
  71.5 1.0 copy-start.15
  78.8 19.4 %copy-start.19 = (f32[8,384]{1,0:T(8,128)S(1)}, f32[8,384]{1,0:T(8,128)}, u32[]{:S(2)}) copy-start(f32[8,384]{1,0:T(8,128)} %param.23) | copy-start | bytes 36868
  78.8 188.4 %all-to-all-start = ((f32[64,40,128]{2,1,0:T(8,128)}), f32[64,40,128]{2,1,0:T(8,128)S(1)}, u32[]{:S(2)}, u32[]{:S(2)}) async-start(f32[64,40,128]{2,1,0:T(8,128)} %bitcast.9), calls=%async_computation | async-start | bytes 2621440 | tf_op jit(solution)/shard_map/all_to_all | solution.py:310
  267.3 1.0 copy-start.8
  268.3 1.0 copy-start.9
  269.3 1.0 copy-start.10
  270.3 1.0 copy-start.11
  275.1 45.7 %all-to-all-start.1 = ((f32[64,40,128]{2,1,0:T(8,128)}), f32[64,40,128]{2,1,0:T(8,128)S(1)}, u32[]{:S(2)}, u32[]{:S(2)}) async-start(f32[64,40,128]{2,1,0:T(8,128)} %shard_map.175), calls=%async_computation.1 | async-start | bytes 2621440 | tf_op jit(solution)/shard_map/all_to_all | solution.py:334
  282.1 169.6 %copy-start.21 = (f32[1,512]{1,0:T(1,128)S(1)}, f32[1,512]{1,0:T(1,128)}, u32[]{:S(2)}) copy-start(f32[1,512]{1,0:T(1,128)} %param.27) | copy-start | bytes 6148
  282.1 169.6 %copy-start.22 = (f32[1,512]{1,0:T(1,128)S(1)}, f32[1,512]{1,0:T(1,128)}, u32[]{:S(2)}) copy-start(f32[1,512]{1,0:T(1,128)} %param.26) | copy-start | bytes 6148
  322.0 0.7 copy-start.12
  322.8 171.4 %collective-permute-start.4 = (f32[6,72,512]{2,1,0:T(8,128)}, f32[6,72,512]{2,1,0:T(8,128)}, u32[]{:S(2)}, u32[]{:S(2)}) collective-permute-start(f32[6,72,512]{2,1,0:T(8,128)} %get-tuple-element.10.own), channel_id=1, source_target_pairs={{0,64},{64,128},{128,192},{192,256},{256,320},{320,384},{384,448},... | collective-permute-start | bytes 2654216 | tf_op jit(solution)/shard_map/ppermute | solution.py:341
  428.5 23.2 %collective-permute-start.5 = (f32[512]{0:T(512)S(1)}, f32[512]{0:T(512)S(1)}, u32[]{:S(2)}, u32[]{:S(2)}) collective-permute-start(f32[512]{0:T(512)S(1)} %slice_select_fusion.1), channel_id=1, source_target_pairs={{1,2},{2,1},{3,4},{4,3},{5,6},{6,5},{7,8},{8,7},{9,10},{10,9},{11,... | collective-permute-start | bytes 6152 | tf_op jit(solution)/shard_map/ppermute | solution.py:313
  451.7 23.2 %collective-permute-start.6 = (f32[512]{0:T(512)S(1)}, f32[512]{0:T(512)S(1)}, u32[]{:S(2)}, u32[]{:S(2)}) collective-permute-start(f32[512]{0:T(512)S(1)} %multiply_select_fusion), channel_id=1, source_target_pairs={{1,2},{2,1},{3,4},{4,3},{5,6},{6,5},{7,8},{8,7},{9,10},{10,9},{11,... | collective-permute-start | bytes 6152 | tf_op jit(solution)/shard_map/ppermute | solution.py:319
  482.2 1.7 copy-start.1
  482.2 1.9 copy-start.2
  484.1 1.0 copy-start.13
  487.9 3.7 collective-permute-start.7

commit v2 on v1

v2 whole, which is shorter than its diff:
```python
import jax
import jax.numpy as jnp
import ml_dtypes
import numpy as np
from jax import lax
from jax.experimental import pallas as pl
from jax.experimental.pallas import tpu as pltpu
from jax.sharding import PartitionSpec as P

LEV, LON, ROWS, KEEP, NLAT, TILES, NWIN = 72, 768, 6, 512, 384, 64, 16
EXT = 8
UNITS = 5
VMEM_LIMIT = 58 * 1024 * 1024
SLOTS = 512
CELL_ROWS = EXT * LEV


def zonal_table():
    half = KEEP // 2
    wave = np.arange(KEEP)
    number = np.where(wave < half, wave, wave - half + 1)
    phase = number[:, None] * np.arange(LON)[None, :] % LON
    angle = 2.0 * np.pi * phase / LON
    scale = np.where(wave == 0, np.sqrt(1.0 / LON), np.sqrt(2.0 / LON))
    return np.where((wave < half)[:, None], np.cos(angle), np.sin(angle)) * scale[:, None]


def meridional_table():
    modes = np.arange(NLAT)
    phase = modes[:, None] * (2 * modes[None, :] + 1) % (4 * NLAT)
    scale = np.where(modes == 0, np.sqrt(1.0 / NLAT), np.sqrt(2.0 / NLAT))
    return np.cos(np.pi * phase / (2.0 * NLAT)) * scale[:, None]


def extended_meridional():
    table = meridional_table()
    out = np.zeros((NLAT, TILES, EXT))
    for tile in range(TILES):
        for i in range(EXT):
            row = tile * ROWS + (i if tile % 2 else ROWS - 1 - i)
            if 0 <= row < NLAT:
                out[:, tile, i] = table[:, row]
    return out.reshape(NLAT, TILES * EXT)


def two_parts(table):
    high = table.astype(ml_dtypes.bfloat16)
    low = (table - high.astype(np.float64)).astype(ml_dtypes.bfloat16)
    return high, low


def split(x):
    high = x.astype(jnp.bfloat16)
    low = (x - high.astype(jnp.float32)).astype(jnp.bfloat16)
    return high, low


def dot(a, b):
    return jnp.dot(a, b, preferred_element_type=jnp.float32)


def dot3(a, b):
    return dot(a[0], b[0]) + (dot(a[0], b[1]) + dot(a[1], b[0]))


def dot_nt(a, b):
    return lax.dot_general(a, b, (((1,), (1,)), ((), ())), preferred_element_type=jnp.float32)


def dot3_nt(a, b):
    return dot_nt(a[0], b[0]) + (dot_nt(a[0], b[1]) + dot_nt(a[1], b[0]))


def weights(a, b, c):
    return 1.0 - 2.0 * a - 2.0 * b, b - 0.5 * c, b + 0.5 * c


def unit_base(i, quarter, block):
    return quarter * 640 + (block % 2) * 40 + (block // 2) * 8 + i


SHIFT, LAMBDA, HALO, PACK_IN, PACK_OUT, OBS, FOUND, DEPART, SPEC, FORCE = range(10)


def kernel(
    inc,
    bg,
    lat,
    lon,
    drift,
    spectrum,
    cells,
    count,
    innovation,
    precision,
    zh,
    zl,
    ph,
    plo,
    qh,
    ql,
    out,
    coefs,
    shifted,
    near,
    pack,
    pack_in,
    pack_out,
    obs,
    obs_far,
    found,
    found_far,
    depart,
    depart_far,
    spec,
    p,
    mid,
    y,
    send,
    got,
    hot_x,
    hot_r,
    lam,
    lam_near,
    force,
    force_near,
    misc_s,
    misc_r,
    spec_s,
    spec_r,
    fwd_s,
    fwd_r,
    bwd_s,
    bwd_r,
    send2,
    got2,
):
    me = lax.axis_index("tile")
    win = lax.axis_index("win")
    core = me % 2
    half = (me // 2) % 2
    xx = (me // 4) % 4
    yy = me // 16
    inside = jnp.logical_and(me > 0, me < TILES - 1)
    partner = me + 1 - 2 * core
    outer = me + 2 * core - 1
    before = (win + NWIN - 1) % NWIN
    after = (win + 1) % NWIN

    def copy(src, dst, ssem, rsem, window, tile):
        return pltpu.make_async_remote_copy(
            src_ref=src,
            dst_ref=dst,
            send_sem=ssem,
            recv_sem=rsem,
            device_id=(window, tile),
            device_id_type=pl.DeviceIdType.MESH,
        )

    def misc(k, src, dst, window, tile):
        return copy(src, dst, misc_s.at[k], misc_r.at[k], window, tile)

    barrier = pltpu.get_barrier_semaphore()

    def greet(j, carry):
        pl.semaphore_signal(
            barrier,
            inc=1,
            device_id=(win, (me + j) % TILES),
            device_id_type=pl.DeviceIdType.MESH,
        )
        return carry

    for window in (before, after):
        pl.semaphore_signal(
            barrier, inc=1, device_id=(window, me), device_id_type=pl.DeviceIdType.MESH
        )
    lax.fori_loop(1, TILES, greet, 0)

    def src(i):
        return core * i + (1 - core) * (ROWS - 1 - i)

    pack[...] = jnp.zeros_like(pack)
    for k, (ref, i) in enumerate(
        ((lat, 0), (lat, 1), (lon, 0), (drift, 0), (lat, 5), (lat, 4), (lon, 5), (drift, 5))
    ):
        pack[k : k + 1, :] = ref[pl.ds(src(i), 1), :]
    spec[xx, half, core] = spectrum[...]

    number = cells[...].astype(jnp.float32)
    level = jnp.floor((number + 0.5) * (1.0 / (ROWS * LON)))
    rest = number - level * (ROWS * LON)
    row = jnp.floor((rest + 0.5) * (1.0 / LON))
    place = jnp.where(core == 0, ROWS - 1 - row, row)
    slot = lax.broadcasted_iota(jnp.int32, (1, SLOTS), 1)
    live = slot < count[...]
    obs[0:1, :] = jnp.where(live, place * LEV + level, -1.0)
    obs[1:2, :] = rest - row * LON

    @pl.when(jnp.logical_not(inside))
    def _():
        pack_out[...] = jnp.zeros_like(pack_out)
        obs_far[...] = jnp.zeros_like(obs_far)
        found_far[...] = jnp.zeros_like(found_far)
        depart_far[...] = jnp.zeros_like(depart_far)

    first = jnp.where(win == 0, 1.0, 0.0).astype(jnp.float32)
    table = (zh[...], zl[...])
    field = inc[...] - first * bg[...]
    own = dot3(split(field.reshape(ROWS * LEV, LON)), table).reshape(ROWS, LEV, KEEP)
    for i in range(ROWS):
        coefs[src(i)] = own[i]

    pl.semaphore_wait(barrier, TILES + 1)

    shift = misc(SHIFT, coefs, shifted, before, me)
    pack_inner = misc(PACK_IN, pack, pack_in, win, partner)
    pack_outer = misc(PACK_OUT, pack, pack_out, win, outer)
    cells_outer = misc(OBS, obs, obs_far, win, outer)
    spec_across = misc(
        SPEC, spec.at[xx, half, core], spec.at[xx, half, core], win, me + 2 - 4 * half
    )
    rim = (1 - core) * (ROWS - 2)
    halo = misc(HALO, inc.at[pl.ds(rim, 2)], near, win, partner)
    pack_inner.start()
    halo.start()

    @pl.when(inside)
    def _():
        pack_outer.start()
        cells_outer.start()

    shift.start()
    spec_across.start()

    pack_inner.wait()
    halo.wait()

    @pl.when(inside)
    def _():
        pack_outer.wait()

    def la(r):
        if r < 0:
            return pack_in[-1 - r : -r, :]
        if r >= ROWS:
            return pack_out[r - 2 : r - 1, :]
        return lat[pl.ds(src(r), 1), :]

    def lo(r):
        if r < 0:
            return pack_in[2:3, :]
        if r >= ROWS:
            return pack_out[6:7, :]
        return lon[pl.ds(src(r), 1), :]

    def dr(r):
        if r < 0:
            return pack_in[3:4, :]
        if r >= ROWS:
            return pack_out[7:8, :]
        return drift[pl.ds(src(r), 1), :]

    def beyond(r):
        return near[core + (1 - 2 * core) * (-1 - r)]

    def state(r):
        return beyond(r) if r < 0 else inc[src(r)]

    def step(get, r, highest):
        a = la(r)
        if r > highest:
            return a * get(r - 1)
        cen, east, west = weights(a, lo(r), dr(r))
        mine = get(r)
        beside = get(r - 1)
        if r < highest:
            beside = beside + get(r + 1)
        return (
            cen * mine
            + a * beside
            + east * pltpu.roll(mine, LON - 1, 1)
            + west * pltpu.roll(mine, 1, 1)
        )

    for r in range(-1, ROWS + 1):
        mid[r + 1] = step(state, r, ROWS - 1)
    for r in range(EXT):
        p[r] = step(lambda q: mid[q + 1], r, ROWS)
    parts = split(p[...].reshape(CELL_ROWS, LON))
    y[...] = dot3(parts, table).reshape(EXT, LEV, KEEP)

    spec_across.wait()

    def spec_copy(j):
        return copy(
            spec.at[xx, :, core],
            spec.at[xx, :, core],
            spec_s.at[j],
            spec_r.at[xx * 2 + core],
            win,
            yy * 16 + (xx + j // 2) % 4 * 4 + half * 2 + (core + j % 2) % 2,
        )

    for j in range(1, 8):
        spec_copy(j).start()

    shift.wait()
    keep = jnp.where(win == NWIN - 1, 0.0, 1.0).astype(jnp.float32)
    for i in range(EXT):
        c = -keep * y[i]
        if i < ROWS:
            c = shifted[i] + c
        for quarter in range(4):
            for block in range(9):
                send[pl.ds(unit_base(i, quarter, block), 8, stride=80), :] = c[
                    block * 8 : block * 8 + 8, quarter * 128 : quarter * 128 + 128
                ]

    def rows_of(core_there):
        return 40 if core_there == 0 else 32

    def block(ref, t, rows):
        return ref.at[pl.ds(t * 40, rows), :]

    def fwd(d, s, rows):
        return copy(block(send, d, rows), block(got, s, rows), fwd_s.at[d], fwd_r.at[s], win, d)

    def bwd(d, s, rows):
        return copy(block(send2, d, rows), block(got2, s, rows), bwd_s.at[d], bwd_r.at[s], win, d)

    def all_tiles(act, dest_core, dh, skip_self):
        def one(j, carry):
            d = (yy + j // 4) % 4 * 16 + (xx + j % 4) % 4 * 4 + (half + dh) % 2 * 2 + dest_core
            if skip_self:
                pl.when(d != me)(lambda: act(d))
            else:
                act(d)
            return carry

        lax.fori_loop(0, 16, one, 0)

    for dh in (1, 0):
        for there in (0, 1):
            rows = rows_of(there)
            all_tiles(lambda d: fwd(d, me, rows).start(), there, dh, dh == 0)
    got[pl.ds(me * 40, 40), :] = send[pl.ds(me * 40, 40), :]

    @pl.when(inside)
    def _():
        cells_outer.wait()

    far_r = obs_far[0:1, :]
    far_r = jnp.where(
        far_r >= 5.0 * LEV, far_r + LEV, jnp.where(far_r >= 4.0 * LEV, far_r + 3.0 * LEV, -1.0)
    )
    spot_r = jnp.concatenate([obs[0:1, :], far_r], axis=1).astype(jnp.int32)
    spot_x = jnp.concatenate([obs[1:2, :], obs_far[1:2, :]], axis=1).astype(jnp.int32)
    one, zero = jnp.float32(1.0), jnp.float32(0.0)
    hot_x[...] = jnp.where(
        lax.broadcasted_iota(jnp.int32, (LON, 2 * SLOTS), 0) == spot_x, one, zero
    ).astype(jnp.bfloat16)
    hot = jnp.where(
        lax.broadcasted_iota(jnp.int32, (CELL_ROWS, 2 * SLOTS), 0) == spot_r, one, zero
    )
    hot_r[...] = hot.astype(jnp.bfloat16)
    parts = split(p[...].reshape(CELL_ROWS, LON))
    picked = dot(parts[0], hot_x[...]) + dot(parts[1], hot_x[...])
    read = jnp.sum(picked * hot, axis=0, keepdims=True)
    found[...] = read[:, SLOTS:]
    found_outer = misc(FOUND, found, found_far, win, outer)
    pl.when(inside)(lambda: found_outer.start())

    for mine in (0, 1):

        @pl.when(core == mine)
        def _():
            for dh in (1, 0):
                for there in (0, 1):
                    all_tiles(
                        lambda s: fwd(s, s, rows_of(mine)).wait_recv(), there, dh, dh == 0
                    )

    pl.when(inside)(lambda: found_outer.wait())
    depart[...] = jnp.where(
        obs[0:1, :] >= 0.0,
        precision[...] * (read[:, :SLOTS] + found_far[...] - innovation[...]),
        0.0,
    )
    depart_outer = misc(DEPART, depart, depart_far, win, outer)
    pl.when(inside)(lambda: depart_outer.start())

    def spec_wait(j):
        there_x, there_c = (xx + j // 2) % 4, (core + j % 2) % 2
        return copy(
            spec.at[there_x, :, there_c],
            spec.at[there_x, :, there_c],
            spec_s.at[j],
            spec_r.at[there_x * 2 + there_c],
            win,
            partner,
        )

    for j in range(1, 8):
        spec_wait(j).wait_recv()
    data = got[...].reshape(TILES, UNITS, EXT, 128)
    x = jnp.concatenate([data[:, u].reshape(TILES * EXT, 128) for u in range(UNITS)], axis=1)
    modal = dot3((ph[...], plo[...]), split(x))
    scale = spec[...].reshape(128, NLAT).T
    modal = modal * jnp.concatenate([scale] * UNITS, axis=1)
    back = dot3((qh[...], ql[...]), split(modal))
    for u in range(UNITS):
        unit = back[:, u * 128 : u * 128 + 128].reshape(TILES, EXT, 128)
        for t in range(TILES):
            send2[t * 40 + u * 8 : t * 40 + u * 8 + 8, :] = unit[t]

    for mine in (0, 1):

        @pl.when(core == mine)
        def _():
            for dh in (1, 0):
                for there in (0, 1):
                    all_tiles(
                        lambda d: bwd(d, me, rows_of(mine)).start(), there, dh, dh == 0
                    )

    got2[pl.ds(me * 40, 40), :] = send2[pl.ds(me * 40, 40), :]

    pl.when(inside)(lambda: depart_outer.wait())
    pushed = jnp.concatenate([depart[...], depart_far[...]], axis=1)
    high, low = split(hot_r[...].astype(jnp.float32) * pushed)
    force[...] = (dot_nt(high, hot_x[...]) + dot_nt(low, hot_x[...])).reshape(EXT, LEV, LON)

    for dh in (1, 0):
        for there in (0, 1):
            rows = rows_of(there)
            all_tiles(lambda s: bwd(s, s, rows).wait_recv(), there, dh, dh == 0)

    for i in range(EXT):
        for quarter in range(4):
            for b in range(9):
                lam[i, b * 8 : b * 8 + 8, quarter * 128 : quarter * 128 + 128] = got2[
                    pl.ds(unit_base(i, quarter, b), 8, stride=80), :
                ]
    passed = misc(LAMBDA, lam.at[pl.ds(0, ROWS)], lam_near, after, me)
    passed.start()

    table = (zh[...], zl[...])
    fields = dot3_nt(split(lam[...].reshape(CELL_ROWS, KEEP)), table).reshape(EXT, LEV, LON)
    force[...] = keep * fields - force[...]
    edge = misc(FORCE, force.at[pl.ds(0, 2)], force_near, win, partner)
    edge.start()
    edge.wait()

    def start(r):
        return force_near[-1 - r] if r < 0 else force[r]

    def back_step(get, r):
        cen, east, west = weights(la(r), lo(r), dr(r))
        mine = get(r)
        return (
            cen * mine
            + la(r + 1) * get(r + 1)
            + la(r - 1) * get(r - 1)
            + pltpu.roll(east * mine, 1, 1)
            + pltpu.roll(west * mine, LON - 1, 1)
        )

    for r in range(-1, ROWS + 1):
        mid[r + 1] = back_step(start, r)
    for r in range(ROWS):
        p[r] = back_step(lambda q: mid[q + 1], r)

    passed.wait()
    fields = dot3_nt(split(lam_near[...].reshape(ROWS * LEV, KEEP)), table)
    fields = fields.reshape(ROWS, LEV, LON)
    for i in range(ROWS):
        out[src(i)] = fields[i] - p[i]

    for there in (0, 1):
        rows = rows_of(there)
        for dh in (1, 0):
            all_tiles(lambda d: fwd(d, me, rows).wait_send(), there, dh, dh == 0)
    for mine in (0, 1):

        @pl.when(core == mine)
        def _():
            for dh in (1, 0):
                for there in (0, 1):
                    all_tiles(
                        lambda d: bwd(d, me, rows_of(mine)).wait_send(), there, dh, dh == 0
                    )

    for j in range(1, 8):
        spec_copy(j).wait_send()


def body(
    increment,
    background,
    lat_diffusion,
    lon_diffusion,
    advection,
    spectrum,
    obs_index,
    obs_count,
    innovation,
    obs_precision,
):
    zonal = two_parts(np.ascontiguousarray(zonal_table().T))
    merid = extended_meridional()
    merid_fwd = two_parts(merid)
    merid_back = two_parts(np.ascontiguousarray(merid.T))
    f32 = jnp.float32
    sems = pltpu.SemaphoreType.DMA
    scratch = [
        ((ROWS, LEV, KEEP), f32),
        ((ROWS, LEV, KEEP), f32),
        ((2, LEV, LON), f32),
        ((8, LON), f32),
        ((8, LON), f32),
        ((8, LON), f32),
        ((2, SLOTS), f32),
        ((2, SLOTS), f32),
        ((1, SLOTS), f32),
        ((1, SLOTS), f32),
        ((1, SLOTS), f32),
        ((1, SLOTS), f32),
        ((4, 2, 2, 8, NLAT), f32),
        ((EXT, LEV, LON), f32),
        ((EXT, LEV, LON), f32),
        ((EXT, LEV, KEEP), f32),
        ((TILES * 40, 128), f32),
        ((TILES * 40, 128), f32),
        ((LON, 2 * SLOTS), jnp.bfloat16),
        ((CELL_ROWS, 2 * SLOTS), jnp.bfloat16),
        ((EXT, LEV, KEEP), f32),
        ((ROWS, LEV, KEEP), f32),
        ((EXT, LEV, LON), f32),
        ((2, LEV, LON), f32),
    ]
    args = (
        increment[0].transpose(1, 0, 2),
        background.transpose(1, 0, 2),
        lat_diffusion[0],
        lon_diffusion[0],
        advection[0],
        spectrum,
        obs_index,
        obs_count,
        innovation,
        obs_precision,
        *zonal,
        *merid_fwd,
        *merid_back,
    )
    vmem = pl.BlockSpec(memory_space=pltpu.VMEM)
    gradient = pl.pallas_call(
        kernel,
        out_shape=jax.ShapeDtypeStruct((ROWS, LEV, LON), f32),
        in_specs=[vmem] * len(args),
        out_specs=vmem,
        scratch_shapes=[pltpu.VMEM(shape, kind) for shape, kind in scratch]
        + [sems((10,)), sems((10,)), sems((8,)), sems((8,))]
        + [sems((TILES,))] * 4
        + [pltpu.VMEM((TILES * 40, 128), f32)] * 2,
        compiler_params=pltpu.CompilerParams(
            vmem_limit_bytes=VMEM_LIMIT, collective_id=0, has_side_effects=True
        ),
    )(*args)
    return gradient.transpose(1, 0, 2)[None]


def solution(mesh):
    in_specs = (
        P("win", None, "tile", None),
        P(None, "tile", None),
        P("win", "tile", None),
        P("win", "tile", None),
        P("win", "tile", None),
        P("tile", None),
        P("win", "tile"),
        P("win", "tile"),
        P("win", "tile"),
        P("win", "tile"),
    )
    out_specs = P("win", None, "tile", None)
    return jax.shard_map(body, mesh=mesh, in_specs=in_specs, out_specs=out_specs, check_vma=False)
```

time: 503 us -> 343 us (0.68)
  the two profiles are of different devices: /device:TPU:1 before, /device:TPU:649 now
where the time goes in v2:
time: 343 us
  Pallas kernels  337 us (98%)
  local copies, waits for them, and re-layouts  5.16 us (2%)
    pallas_call x1, Pallas kernels, body(): pl.pallas_call(kernel, out_shape=jax.ShapeDtypeStruct((ROWS, LEV, LON), f...  337 us

profile of v2, /device:TPU:649, one launch (start us, length us, event | category | flops | bytes accessed | tf_op | source)
XLA Modules:
  0.0 342.8 jit_solution(4446094927961857828)
XLA Ops:
  0.7 1.3 copy.23
  2.0 1.4 copy_bitcast_fusion
  3.3 336.9 %shard_map.154 = f32[6,72,768]{2,1,0:T(8,128)} custom-call(f32[6,72,768]{2,1,0:T(8,128)} %bitcast.15, f32[6,72,768]{2,1,0:T(8,128)} %bitcast.16, f32[6,768]{1,0:T(8,128)} %bitcast.17, f32[6,768]{1,0:T(8,128)} %get-tuple-element.6.lon, f32[6,768]{1,0:T(8,128)} %get-tuple-element.5.drift, f32[8,384]{1,0:T(8,128)} %spectrum.1, s32[1,512]{1,0:T(1,128)} %cells.1, ...), custom_call_target="tpu_custom_call" | custom-call | tf_op jit(solution)/shard_map/pallas_call | solution.py:558
  340.3 2.5 copy.26

commit v3 on v2

--- a/solution.py
+++ b/solution.py
@@ -9,7 +9,6 @@
 
 LEV, LON, ROWS, KEEP, NLAT, TILES, NWIN = 72, 768, 6, 512, 384, 64, 16
 EXT = 8
-UNITS = 5
 VMEM_LIMIT = 58 * 1024 * 1024
 SLOTS = 512
 CELL_ROWS = EXT * LEV
@@ -75,11 +74,28 @@
     return 1.0 - 2.0 * a - 2.0 * b, b - 0.5 * c, b + 0.5 * c
 
 
-def unit_base(i, quarter, block):
-    return quarter * 640 + (block % 2) * 40 + (block // 2) * 8 + i
-
-
-SHIFT, LAMBDA, HALO, PACK_IN, PACK_OUT, OBS, FOUND, DEPART, SPEC, FORCE = range(10)
+CHUNKS, DEEP = 3, LEV // 3
+OWNER = (((0, 0), (0, 1), (1, 0)), ((0, 0), (1, 0), (1, 1)), ((0, 0), (0, 1), (1, 0)))
+SPAN = 16
+PART = TILES * SPAN
+
+
+def unit_base(i, quarter, chunk, j):
+    core, unit = OWNER[chunk][j]
+    return chunk * PART + quarter * 16 * SPAN + core * SPAN + unit * 8 + i
+
+
+def rows_of(chunk, core):
+    return 8 * sum(owner == core for owner, _ in OWNER[chunk])
+
+
+def rows_mixed(chunk, mine):
+    return 32 * (rows_of(chunk, 0) + rows_of(chunk, 1)) - rows_of(chunk, mine)
+
+
+HALO, PACK_IN, PACK_OUT, OBS, FOUND, DEPART, SPEC = range(7)
+SHIFT, LAMBDA, FORCE = 7, 10, 13
+MISC = 16
 
 
 def kernel(
@@ -184,7 +200,7 @@
     for k, (ref, i) in enumerate(
         ((lat, 0), (lat, 1), (lon, 0), (drift, 0), (lat, 5), (lat, 4), (lon, 5), (drift, 5))
     ):
-        pack[k : k + 1, :] = ref[pl.ds(src(i), 1), :]
+        pack[k : k + 1, :] = ref[src(i)]
     spec[xx, half, core] = spectrum[...]
 
     number = cells[...].astype(jnp.float32)
@@ -206,14 +222,16 @@
 
     first = jnp.where(win == 0, 1.0, 0.0).astype(jnp.float32)
     table = (zh[...], zl[...])
-    field = inc[...] - first * bg[...]
-    own = dot3(split(field.reshape(ROWS * LEV, LON)), table).reshape(ROWS, LEV, KEEP)
-    for i in range(ROWS):
-        coefs[src(i)] = own[i]
+    for n in range(CHUNKS):
+        deep = pl.ds(n * DEEP, DEEP)
+        field = inc[:, deep, :] - first * bg[:, deep, :]
+        own = dot3(split(field.reshape(ROWS * DEEP, LON)), table).reshape(ROWS, DEEP, KEEP)
+        for i in range(ROWS):
+            coefs[n, src(i)] = own[i]
 
     pl.semaphore_wait(barrier, TILES + 1)
 
-    shift = misc(SHIFT, coefs, shifted, before, me)
+    shift = [misc(SHIFT + n, coefs.at[n], shifted.at[n], before, me) for n in range(CHUNKS)]
     pack_inner = misc(PACK_IN, pack, pack_in, win, partner)
     pack_outer = misc(PACK_OUT, pack, pack_out, win, outer)
     cells_outer = misc(OBS, obs, obs_far, win, outer)
@@ -230,8 +248,10 @@
         pack_outer.start()
         cells_outer.start()
 
-    shift.start()
+    shift[0].start()
     spec_across.start()
+    shift[1].start()
+    shift[2].start()
 
     pack_inner.wait()
     halo.wait()
@@ -245,21 +265,21 @@
             return pack_in[-1 - r : -r, :]
         if r >= ROWS:
             return pack_out[r - 2 : r - 1, :]
-        return lat[pl.ds(src(r), 1), :]
+        return lat[src(r)]
 
     def lo(r):
         if r < 0:
             return pack_in[2:3, :]
         if r >= ROWS:
             return pack_out[6:7, :]
-        return lon[pl.ds(src(r), 1), :]
+        return lon[src(r)]
 
     def dr(r):
         if r < 0:
             return pack_in[3:4, :]
         if r >= ROWS:
             return pack_out[7:8, :]
-        return drift[pl.ds(src(r), 1), :]
+        return drift[src(r)]
 
     def beyond(r):
         return near[core + (1 - 2 * core) * (-1 - r)]
@@ -290,8 +310,6 @@
     parts = split(p[...].reshape(CELL_ROWS, LON))
     y[...] = dot3(parts, table).reshape(EXT, LEV, KEEP)
 
-    spec_across.wait()
-
     def spec_copy(j):
         return copy(
             spec.at[xx, :, core],
@@ -302,37 +320,40 @@
             yy * 16 + (xx + j // 2) % 4 * 4 + half * 2 + (core + j % 2) % 2,
         )
 
-    for j in range(1, 8):
-        spec_copy(j).start()
-
-    shift.wait()
     keep = jnp.where(win == NWIN - 1, 0.0, 1.0).astype(jnp.float32)
-    for i in range(EXT):
-        c = -keep * y[i]
-        if i < ROWS:
-            c = shifted[i] + c
-        for quarter in range(4):
-            for block in range(9):
-                send[pl.ds(unit_base(i, quarter, block), 8, stride=80), :] = c[
-                    block * 8 : block * 8 + 8, quarter * 128 : quarter * 128 + 128
-                ]
-
-    def rows_of(core_there):
-        return 40 if core_there == 0 else 32
-
-    def block(ref, t, rows):
-        return ref.at[pl.ds(t * 40, rows), :]
-
-    def fwd(d, s, rows):
-        return copy(block(send, d, rows), block(got, s, rows), fwd_s.at[d], fwd_r.at[s], win, d)
-
-    def bwd(d, s, rows):
-        return copy(block(send2, d, rows), block(got2, s, rows), bwd_s.at[d], bwd_r.at[s], win, d)
-
-    def all_tiles(act, dest_core, dh, skip_self):
+
+    def arrange(n):
+        for i in range(EXT):
+            c = -keep * y[i, n * DEEP : (n + 1) * DEEP, :]
+            if i < ROWS:
+                c = shifted[n, i] + c
+            for quarter in range(4):
+                for j in range(3):
+                    send[pl.ds(unit_base(i, quarter, n, j), 8, stride=2 * SPAN), :] = c[
+                        j * 8 : j * 8 + 8, quarter * 128 : quarter * 128 + 128
+                    ]
+
+    def block(ref, n, t, rows):
+        return ref.at[pl.ds(n * PART + t * SPAN, rows), :]
+
+    def fwd(n, d, rows):
+        return copy(
+            block(send, n, d, rows), block(got, n, me, rows), fwd_s.at[n], fwd_r.at[n], win, d
+        )
+
+    def bwd(n, d, rows):
+        return copy(
+            block(send2, n, d, rows), block(got2, n, me, rows), bwd_s.at[n], bwd_r.at[n], win, d
+        )
+
+    def total(ref, ref2, ssem, rsem, n, rows):
+        whole = pl.ds(n * PART, rows)
+        return copy(ref.at[whole, :], ref2.at[whole, :], ssem.at[n], rsem.at[n], win, partner)
+
+    def all_tiles(act, dest_core, dh):
         def one(j, carry):
             d = (yy + j // 4) % 4 * 16 + (xx + j % 4) % 4 * 4 + (half + dh) % 2 * 2 + dest_core
-            if skip_self:
+            if dh == 0:
                 pl.when(d != me)(lambda: act(d))
             else:
                 act(d)
@@ -340,11 +361,48 @@
 
         lax.fori_loop(0, 16, one, 0)
 
-    for dh in (1, 0):
-        for there in (0, 1):
-            rows = rows_of(there)
-            all_tiles(lambda d: fwd(d, me, rows).start(), there, dh, dh == 0)
-    got[pl.ds(me * 40, 40), :] = send[pl.ds(me * 40, 40), :]
+    def send_fwd(n):
+        for dh in (1, 0):
+            for there in (0, 1):
+                all_tiles(lambda d: fwd(n, d, rows_of(n, there)).start(), there, dh)
+        own_block = pl.ds(n * PART + me * SPAN, SPAN)
+        got[own_block, :] = send[own_block, :]
+
+    def send_bwd(n):
+        for mine in (0, 1):
+
+            @pl.when(core == mine)
+            def _():
+                for dh in (1, 0):
+                    for there in (0, 1):
+                        all_tiles(lambda d: bwd(n, d, rows_of(n, mine)).start(), there, dh)
+
+        own_block = pl.ds(n * PART + me * SPAN, SPAN)
+        got2[own_block, :] = send2[own_block, :]
+
+    def by_core(act):
+        for mine in (0, 1):
+            pl.when(core == mine)(lambda: act(mine))
+
+    def wait_fwd(n):
+        by_core(
+            lambda mine: total(
+                send, got, fwd_s, fwd_r, n, (TILES - 1) * rows_of(n, mine)
+            ).wait_recv()
+        )
+
+    def wait_bwd(n):
+        by_core(
+            lambda mine: total(send2, got2, bwd_s, bwd_r, n, rows_mixed(n, mine)).wait_recv()
+        )
+
+    shift[0].wait()
+    arrange(0)
+    send_fwd(0)
+
+    spec_across.wait()
+    for j in range(1, 8):
+        spec_copy(j).start()
 
     @pl.when(inside)
     def _():
@@ -354,37 +412,35 @@
     far_r = jnp.where(
         far_r >= 5.0 * LEV, far_r + LEV, jnp.where(far_r >= 4.0 * LEV, far_r + 3.0 * LEV, -1.0)
     )
-    spot_r = jnp.concatenate([obs[0:1, :], far_r], axis=1).astype(jnp.int32)
-    spot_x = jnp.concatenate([obs[1:2, :], obs_far[1:2, :]], axis=1).astype(jnp.int32)
     one, zero = jnp.float32(1.0), jnp.float32(0.0)
-    hot_x[...] = jnp.where(
-        lax.broadcasted_iota(jnp.int32, (LON, 2 * SLOTS), 0) == spot_x, one, zero
-    ).astype(jnp.bfloat16)
-    hot = jnp.where(
-        lax.broadcasted_iota(jnp.int32, (CELL_ROWS, 2 * SLOTS), 0) == spot_r, one, zero
-    )
-    hot_r[...] = hot.astype(jnp.bfloat16)
-    parts = split(p[...].reshape(CELL_ROWS, LON))
-    picked = dot(parts[0], hot_x[...]) + dot(parts[1], hot_x[...])
-    read = jnp.sum(picked * hot, axis=0, keepdims=True)
-    found[...] = read[:, SLOTS:]
+
+    def hot(spots, size):
+        spots = spots.astype(jnp.int32)
+        numbers = lax.broadcasted_iota(jnp.int32, (size, SLOTS), 0)
+        return jnp.where(numbers == spots, one, zero)
+
+    def read(rows, longitudes, lanes):
+        hot_x[:, lanes] = hot(longitudes, LON).astype(jnp.bfloat16)
+        at = hot(rows, CELL_ROWS)
+        hot_r[:, lanes] = at.astype(jnp.bfloat16)
+        parts = split(p[...].reshape(CELL_ROWS, LON))
+        picked = dot(parts[0], hot_x[:, lanes]) + dot(parts[1], hot_x[:, lanes])
+        return jnp.sum(picked * at, axis=0, keepdims=True)
+
+    found[...] = read(far_r, obs_far[1:2, :], slice(SLOTS, 2 * SLOTS))
     found_outer = misc(FOUND, found, found_far, win, outer)
     pl.when(inside)(lambda: found_outer.start())
 
-    for mine in (0, 1):
-
-        @pl.when(core == mine)
-        def _():
-            for dh in (1, 0):
-                for there in (0, 1):
-                    all_tiles(
-                        lambda s: fwd(s, s, rows_of(mine)).wait_recv(), there, dh, dh == 0
-                    )
-
+    for n in (1, 2):
+        shift[n].wait()
+        arrange(n)
+        send_fwd(n)
+
+    depart[...] = read(obs[0:1, :], obs[1:2, :], slice(0, SLOTS))
     pl.when(inside)(lambda: found_outer.wait())
     depart[...] = jnp.where(
         obs[0:1, :] >= 0.0,
-        precision[...] * (read[:, :SLOTS] + found_far[...] - innovation[...]),
+        precision[...] * (depart[...] + found_far[...] - innovation[...]),
         0.0,
     )
     depart_outer = misc(DEPART, depart, depart_far, win, outer)
@@ -403,57 +459,26 @@
 
     for j in range(1, 8):
         spec_wait(j).wait_recv()
-    data = got[...].reshape(TILES, UNITS, EXT, 128)
-    x = jnp.concatenate([data[:, u].reshape(TILES * EXT, 128) for u in range(UNITS)], axis=1)
-    modal = dot3((ph[...], plo[...]), split(x))
     scale = spec[...].reshape(128, NLAT).T
-    modal = modal * jnp.concatenate([scale] * UNITS, axis=1)
-    back = dot3((qh[...], ql[...]), split(modal))
-    for u in range(UNITS):
-        unit = back[:, u * 128 : u * 128 + 128].reshape(TILES, EXT, 128)
-        for t in range(TILES):
-            send2[t * 40 + u * 8 : t * 40 + u * 8 + 8, :] = unit[t]
-
-    for mine in (0, 1):
-
-        @pl.when(core == mine)
-        def _():
-            for dh in (1, 0):
-                for there in (0, 1):
-                    all_tiles(
-                        lambda d: bwd(d, me, rows_of(mine)).start(), there, dh, dh == 0
-                    )
-
-    got2[pl.ds(me * 40, 40), :] = send2[pl.ds(me * 40, 40), :]
-
-    pl.when(inside)(lambda: depart_outer.wait())
-    pushed = jnp.concatenate([depart[...], depart_far[...]], axis=1)
-    high, low = split(hot_r[...].astype(jnp.float32) * pushed)
-    force[...] = (dot_nt(high, hot_x[...]) + dot_nt(low, hot_x[...])).reshape(EXT, LEV, LON)
-
-    for dh in (1, 0):
-        for there in (0, 1):
-            rows = rows_of(there)
-            all_tiles(lambda s: bwd(s, s, rows).wait_recv(), there, dh, dh == 0)
-
-    for i in range(EXT):
-        for quarter in range(4):
-            for b in range(9):
-                lam[i, b * 8 : b * 8 + 8, quarter * 128 : quarter * 128 + 128] = got2[
-                    pl.ds(unit_base(i, quarter, b), 8, stride=80), :
-                ]
-    passed = misc(LAMBDA, lam.at[pl.ds(0, ROWS)], lam_near, after, me)
-    passed.start()
-
-    table = (zh[...], zl[...])
-    fields = dot3_nt(split(lam[...].reshape(CELL_ROWS, KEEP)), table).reshape(EXT, LEV, LON)
-    force[...] = keep * fields - force[...]
-    edge = misc(FORCE, force.at[pl.ds(0, 2)], force_near, win, partner)
-    edge.start()
-    edge.wait()
-
-    def start(r):
-        return force_near[-1 - r] if r < 0 else force[r]
+    scale = jnp.concatenate([scale, scale], axis=1)
+    for n in range(CHUNKS):
+        wait_fwd(n)
+        data = got[n * PART : (n + 1) * PART, :].reshape(TILES, 2, EXT, 128)
+        x = jnp.concatenate([data[:, u].reshape(TILES * EXT, 128) for u in (0, 1)], axis=1)
+        modal = dot3((ph[...], plo[...]), split(x)) * scale
+        back = dot3((qh[...], ql[...]), split(modal))
+        for u in (0, 1):
+            unit = back[:, u * 128 : u * 128 + 128].reshape(TILES, EXT, 128)
+            for t in range(TILES):
+                at = n * PART + t * SPAN + u * 8
+                send2[at : at + 8, :] = unit[t]
+        send_bwd(n)
+        if n == 1:
+            pl.when(inside)(lambda: depart_outer.wait())
+            pushed = jnp.concatenate([depart[...], depart_far[...]], axis=1)
+            high, low = split(hot_r[...].astype(jnp.float32) * pushed)
+            placed = dot_nt(high, hot_x[...]) + dot_nt(low, hot_x[...])
+            force[...] = placed.reshape(EXT, LEV, LON)
 
     def back_step(get, r):
         cen, east, west = weights(la(r), lo(r), dr(r))
@@ -466,31 +491,75 @@
             + pltpu.roll(west * mine, LON - 1, 1)
         )
 
-    for r in range(-1, ROWS + 1):
-        mid[r + 1] = back_step(start, r)
-    for r in range(ROWS):
-        p[r] = back_step(lambda q: mid[q + 1], r)
-
-    passed.wait()
-    fields = dot3_nt(split(lam_near[...].reshape(ROWS * LEV, KEEP)), table)
-    fields = fields.reshape(ROWS, LEV, LON)
-    for i in range(ROWS):
-        out[src(i)] = fields[i] - p[i]
-
-    for there in (0, 1):
-        rows = rows_of(there)
-        for dh in (1, 0):
-            all_tiles(lambda d: fwd(d, me, rows).wait_send(), there, dh, dh == 0)
-    for mine in (0, 1):
-
-        @pl.when(core == mine)
-        def _():
-            for dh in (1, 0):
-                for there in (0, 1):
-                    all_tiles(
-                        lambda d: bwd(d, me, rows_of(mine)).wait_send(), there, dh, dh == 0
-                    )
-
+    passed = [
+        misc(LAMBDA + n, lam.at[n, pl.ds(0, ROWS)], lam_near.at[n], after, me)
+        for n in range(CHUNKS)
+    ]
+    edge = [
+        misc(
+            FORCE + n,
+            force.at[pl.ds(0, 2), pl.ds(n * DEEP, DEEP), :],
+            force_near.at[:, pl.ds(n * DEEP, DEEP), :],
+            win,
+            partner,
+        )
+        for n in range(CHUNKS)
+    ]
+
+    def receive(n):
+        wait_bwd(n)
+        for i in range(EXT):
+            for quarter in range(4):
+                for j in range(3):
+                    lam[n, i, j * 8 : j * 8 + 8, quarter * 128 : quarter * 128 + 128] = got2[
+                        pl.ds(unit_base(i, quarter, n, j), 8, stride=2 * SPAN), :
+                    ]
+        passed[n].start()
+        fields = dot3_nt(split(lam[n].reshape(EXT * DEEP, KEEP)), (zh[...], zl[...]))
+        fields = keep * fields.reshape(EXT, DEEP, LON)
+        deep = pl.ds(n * DEEP, DEEP)
+        force[:, deep, :] = fields - force[:, deep, :]
+        edge[n].start()
+
+    def adjoint(n):
+        edge[n].wait()
+        deep = pl.ds(n * DEEP, DEEP)
+
+        def start(r):
+            return force_near[-1 - r, deep, :] if r < 0 else force[r, deep, :]
+
+        for r in range(-1, ROWS + 1):
+            mid[r + 1, deep, :] = back_step(start, r)
+        for r in range(ROWS):
+            p[r, deep, :] = back_step(lambda q: mid[q + 1, deep, :], r)
+
+    def finish(n):
+        passed[n].wait()
+        deep = pl.ds(n * DEEP, DEEP)
+        fields = dot3_nt(split(lam_near[n].reshape(ROWS * DEEP, KEEP)), (zh[...], zl[...]))
+        fields = fields.reshape(ROWS, DEEP, LON)
+        for i in range(ROWS):
+            out[src(i), deep, :] = fields[i] - p[i, deep, :]
+
+    receive(0)
+    adjoint(0)
+    receive(1)
+    adjoint(1)
+    finish(0)
+    receive(2)
+    finish(1)
+    adjoint(2)
+    finish(2)
+
+    for n in range(CHUNKS):
+        by_core(
+            lambda mine: total(send, got, fwd_s, fwd_r, n, rows_mixed(n, mine)).wait_send()
+        )
+        by_core(
+            lambda mine: total(
+                send2, got2, bwd_s, bwd_r, n, (TILES - 1) * rows_of(n, mine)
+            ).wait_send()
+        )
     for j in range(1, 8):
         spec_copy(j).wait_send()
 
@@ -514,8 +583,8 @@
     f32 = jnp.float32
     sems = pltpu.SemaphoreType.DMA
     scratch = [
-        ((ROWS, LEV, KEEP), f32),
-        ((ROWS, LEV, KEEP), f32),
+        ((CHUNKS, ROWS, DEEP, KEEP), f32),
+        ((CHUNKS, ROWS, DEEP, KEEP), f32),
         ((2, LEV, LON), f32),
         ((8, LON), f32),
         ((8, LON), f32),
@@ -530,21 +599,21 @@
         ((EXT, LEV, LON), f32),
         ((EXT, LEV, LON), f32),
         ((EXT, LEV, KEEP), f32),
-        ((TILES * 40, 128), f32),
-        ((TILES * 40, 128), f32),
+        ((CHUNKS * PART, 128), f32),
+        ((CHUNKS * PART, 128), f32),
         ((LON, 2 * SLOTS), jnp.bfloat16),
         ((CELL_ROWS, 2 * SLOTS), jnp.bfloat16),
-        ((EXT, LEV, KEEP), f32),
-        ((ROWS, LEV, KEEP), f32),
+        ((CHUNKS, EXT, DEEP, KEEP), f32),
+        ((CHUNKS, ROWS, DEEP, KEEP), f32),
         ((EXT, LEV, LON), f32),
         ((2, LEV, LON), f32),
     ]
     args = (
         increment[0].transpose(1, 0, 2),
         background.transpose(1, 0, 2),
-        lat_diffusion[0],
-        lon_diffusion[0],
-        advection[0],
+        lat_diffusion.transpose(1, 0, 2),
+        lon_diffusion.transpose(1, 0, 2),
+        advection.transpose(1, 0, 2),
         spectrum,
         obs_index,
         obs_count,
@@ -561,9 +630,9 @@
         in_specs=[vmem] * len(args),
         out_specs=vmem,
         scratch_shapes=[pltpu.VMEM(shape, kind) for shape, kind in scratch]
-        + [sems((10,)), sems((10,)), sems((8,)), sems((8,))]
-        + [sems((TILES,))] * 4
-        + [pltpu.VMEM((TILES * 40, 128), f32)] * 2,
+        + [sems((MISC,)), sems((MISC,)), sems((8,)), sems((8,))]
+        + [sems((CHUNKS,))] * 4
+        + [pltpu.VMEM((CHUNKS * PART, 128), f32)] * 2,
         compiler_params=pltpu.CompilerParams(
             vmem_limit_bytes=VMEM_LIMIT, collective_id=0, has_side_effects=True
         ),

time: 343 us -> 313 us (0.913)
  the two profiles are of different devices: /device:TPU:649 before, /device:TPU:1 now
where the time goes in v3:
time: 313 us; the launch traced here: 311 us
  Pallas kernels  308 us (98%)
    pallas_call x1, Pallas kernels, body(): pl.pallas_call(kernel, out_shape=jax.ShapeDtypeStruct((ROWS, LEV, LON), f...  308 us

profile of v3, /device:TPU:1, one launch (start us, length us, event | category | flops | bytes accessed | tf_op | source)
XLA Modules:
  0.0 310.9 jit_solution(10149078893583846524)
XLA Ops:
  0.7 307.8 %shard_map.154 = f32[6,72,768]{2,1,0:T(8,128)} custom-call(f32[6,72,768]{2,1,0:T(8,128)} %bitcast.11, f32[6,72,768]{2,1,0:T(8,128)} %bitcast.12, f32[6,1,768]{2,1,0:T(1,128)} %bitcast.13, f32[6,1,768]{2,1,0:T(1,128)} %bitcast.14, f32[6,1,768]{2,1,0:T(1,128)} %bitcast.15, f32[8,384]{1,0:T(8,128)} %spectrum.1, s32[1,512]{1,0:T(1,128)} %cells.1, ...), custom_call_target="tpu_custom_call" | custom-call | tf_op jit(solution)/shard_map/pallas_call | solution.py:627
  308.4 2.5 copy.19

commit v4 on v3

--- a/solution.py
+++ b/solution.py
@@ -74,15 +74,19 @@
     return 1.0 - 2.0 * a - 2.0 * b, b - 0.5 * c, b + 0.5 * c
 
 
-CHUNKS, DEEP = 3, LEV // 3
-OWNER = (((0, 0), (0, 1), (1, 0)), ((0, 0), (1, 0), (1, 1)), ((0, 0), (0, 1), (1, 0)))
-SPAN = 16
-PART = TILES * SPAN
+OWNER = (((0, 0), (1, 0)), ((0, 0), (0, 1), (0, 2), (1, 0), (1, 1)), ((0, 0), (1, 0)))
+CHUNKS = len(OWNER)
+DEEP = tuple(8 * len(owners) for owners in OWNER)
+LEVEL0 = tuple(sum(DEEP[:n]) for n in range(CHUNKS))
+WIDE = tuple(1 + max(unit for _, unit in owners) for owners in OWNER)
+SPAN = tuple(8 * wide for wide in WIDE)
+PART0 = tuple(TILES * sum(SPAN[:n]) for n in range(CHUNKS))
+BLOCKS = TILES * sum(SPAN)
 
 
 def unit_base(i, quarter, chunk, j):
     core, unit = OWNER[chunk][j]
-    return chunk * PART + quarter * 16 * SPAN + core * SPAN + unit * 8 + i
+    return PART0[chunk] + (quarter * 16 + core) * SPAN[chunk] + unit * 8 + i
 
 
 def rows_of(chunk, core):
@@ -131,7 +135,6 @@
     spec,
     p,
     mid,
-    y,
     send,
     got,
     hot_x,
@@ -223,15 +226,21 @@
     first = jnp.where(win == 0, 1.0, 0.0).astype(jnp.float32)
     table = (zh[...], zl[...])
     for n in range(CHUNKS):
-        deep = pl.ds(n * DEEP, DEEP)
+        deep = pl.ds(LEVEL0[n], DEEP[n])
         field = inc[:, deep, :] - first * bg[:, deep, :]
-        own = dot3(split(field.reshape(ROWS * DEEP, LON)), table).reshape(ROWS, DEEP, KEEP)
+        own = dot3(split(field.reshape(ROWS * DEEP[n], LON)), table)
+        own = own.reshape(ROWS, DEEP[n], KEEP)
         for i in range(ROWS):
-            coefs[n, src(i)] = own[i]
+            coefs[pl.ds(ROWS * LEVEL0[n] + src(i) * DEEP[n], DEEP[n]), :] = own[i]
 
     pl.semaphore_wait(barrier, TILES + 1)
 
-    shift = [misc(SHIFT + n, coefs.at[n], shifted.at[n], before, me) for n in range(CHUNKS)]
+    def six(ref, n):
+        return ref.at[pl.ds(ROWS * LEVEL0[n], ROWS * DEEP[n]), :]
+
+    shift = [
+        misc(SHIFT + n, six(coefs, n), six(shifted, n), before, me) for n in range(CHUNKS)
+    ]
     pack_inner = misc(PACK_IN, pack, pack_in, win, partner)
     pack_outer = misc(PACK_OUT, pack, pack_out, win, outer)
     cells_outer = misc(OBS, obs, obs_far, win, outer)
@@ -307,9 +316,6 @@
         mid[r + 1] = step(state, r, ROWS - 1)
     for r in range(EXT):
         p[r] = step(lambda q: mid[q + 1], r, ROWS)
-    parts = split(p[...].reshape(CELL_ROWS, LON))
-    y[...] = dot3(parts, table).reshape(EXT, LEV, KEEP)
-
     def spec_copy(j):
         return copy(
             spec.at[xx, :, core],
@@ -323,18 +329,22 @@
     keep = jnp.where(win == NWIN - 1, 0.0, 1.0).astype(jnp.float32)
 
     def arrange(n):
+        rows = p[:, LEVEL0[n] : LEVEL0[n] + DEEP[n], :].reshape(EXT * DEEP[n], LON)
+        y = dot3(split(rows), (zh[...], zl[...])).reshape(EXT, DEEP[n], KEEP)
+        shift[n].wait()
         for i in range(EXT):
-            c = -keep * y[i, n * DEEP : (n + 1) * DEEP, :]
+            c = -keep * y[i]
             if i < ROWS:
-                c = shifted[n, i] + c
+                at = ROWS * LEVEL0[n] + i * DEEP[n]
+                c = shifted[at : at + DEEP[n], :] + c
             for quarter in range(4):
-                for j in range(3):
-                    send[pl.ds(unit_base(i, quarter, n, j), 8, stride=2 * SPAN), :] = c[
+                for j in range(len(OWNER[n])):
+                    send[pl.ds(unit_base(i, quarter, n, j), 8, stride=2 * SPAN[n]), :] = c[
                         j * 8 : j * 8 + 8, quarter * 128 : quarter * 128 + 128
                     ]
 
     def block(ref, n, t, rows):
-        return ref.at[pl.ds(n * PART + t * SPAN, rows), :]
+        return ref.at[pl.ds(PART0[n] + t * SPAN[n], rows), :]
 
     def fwd(n, d, rows):
         return copy(
@@ -347,38 +357,36 @@
         )
 
     def total(ref, ref2, ssem, rsem, n, rows):
-        whole = pl.ds(n * PART, rows)
+        whole = pl.ds(PART0[n], rows)
         return copy(ref.at[whole, :], ref2.at[whole, :], ssem.at[n], rsem.at[n], win, partner)
 
-    def all_tiles(act, dest_core, dh):
+    def all_tiles(act, there):
         def one(j, carry):
-            d = (yy + j // 4) % 4 * 16 + (xx + j % 4) % 4 * 4 + (half + dh) % 2 * 2 + dest_core
-            if dh == 0:
-                pl.when(d != me)(lambda: act(d))
-            else:
-                act(d)
+            chip = (yy + j // 4) % 4 * 16 + (xx + j % 4) % 4 * 4 + there
+            act(chip + (1 - half) * 2)
+            close = chip + half * 2
+            pl.when(close != me)(lambda: act(close))
             return carry
 
         lax.fori_loop(0, 16, one, 0)
 
+    def own_block(n):
+        return pl.ds(PART0[n] + me * SPAN[n], SPAN[n])
+
     def send_fwd(n):
-        for dh in (1, 0):
-            for there in (0, 1):
-                all_tiles(lambda d: fwd(n, d, rows_of(n, there)).start(), there, dh)
-        own_block = pl.ds(n * PART + me * SPAN, SPAN)
-        got[own_block, :] = send[own_block, :]
+        for there in (0, 1):
+            all_tiles(lambda d: fwd(n, d, rows_of(n, there)).start(), there)
+        got[own_block(n), :] = send[own_block(n), :]
 
     def send_bwd(n):
         for mine in (0, 1):
 
             @pl.when(core == mine)
             def _():
-                for dh in (1, 0):
-                    for there in (0, 1):
-                        all_tiles(lambda d: bwd(n, d, rows_of(n, mine)).start(), there, dh)
-
-        own_block = pl.ds(n * PART + me * SPAN, SPAN)
-        got2[own_block, :] = send2[own_block, :]
+                for there in (0, 1):
+                    all_tiles(lambda d: bwd(n, d, rows_of(n, mine)).start(), there)
+
+        got2[own_block(n), :] = send2[own_block(n), :]
 
     def by_core(act):
         for mine in (0, 1):
@@ -396,7 +404,6 @@
             lambda mine: total(send2, got2, bwd_s, bwd_r, n, rows_mixed(n, mine)).wait_recv()
         )
 
-    shift[0].wait()
     arrange(0)
     send_fwd(0)
 
@@ -432,7 +439,6 @@
     pl.when(inside)(lambda: found_outer.start())
 
     for n in (1, 2):
-        shift[n].wait()
         arrange(n)
         send_fwd(n)
 
@@ -460,17 +466,19 @@
     for j in range(1, 8):
         spec_wait(j).wait_recv()
     scale = spec[...].reshape(128, NLAT).T
-    scale = jnp.concatenate([scale, scale], axis=1)
     for n in range(CHUNKS):
         wait_fwd(n)
-        data = got[n * PART : (n + 1) * PART, :].reshape(TILES, 2, EXT, 128)
-        x = jnp.concatenate([data[:, u].reshape(TILES * EXT, 128) for u in (0, 1)], axis=1)
-        modal = dot3((ph[...], plo[...]), split(x)) * scale
+        units = range(WIDE[n])
+        data = got[PART0[n] : PART0[n] + TILES * SPAN[n], :]
+        data = data.reshape(TILES, WIDE[n], EXT, 128)
+        x = jnp.concatenate([data[:, u].reshape(TILES * EXT, 128) for u in units], axis=1)
+        modal = dot3((ph[...], plo[...]), split(x))
+        modal = modal * jnp.concatenate([scale] * WIDE[n], axis=1)
         back = dot3((qh[...], ql[...]), split(modal))
-        for u in (0, 1):
+        for u in units:
             unit = back[:, u * 128 : u * 128 + 128].reshape(TILES, EXT, 128)
             for t in range(TILES):
-                at = n * PART + t * SPAN + u * 8
+                at = PART0[n] + t * SPAN[n] + u * 8
                 send2[at : at + 8, :] = unit[t]
         send_bwd(n)
         if n == 1:
@@ -492,14 +500,20 @@
         )
 
     passed = [
-        misc(LAMBDA + n, lam.at[n, pl.ds(0, ROWS)], lam_near.at[n], after, me)
+        misc(
+            LAMBDA + n,
+            lam.at[pl.ds(EXT * LEVEL0[n], ROWS * DEEP[n]), :],
+            six(lam_near, n),
+            after,
+            me,
+        )
         for n in range(CHUNKS)
     ]
     edge = [
         misc(
             FORCE + n,
-            force.at[pl.ds(0, 2), pl.ds(n * DEEP, DEEP), :],
-            force_near.at[:, pl.ds(n * DEEP, DEEP), :],
+            force.at[pl.ds(0, 2), pl.ds(LEVEL0[n], DEEP[n]), :],
+            force_near.at[:, pl.ds(LEVEL0[n], DEEP[n]), :],
             win,
             partner,
         )
@@ -510,20 +524,22 @@
         wait_bwd(n)
         for i in range(EXT):
             for quarter in range(4):
-                for j in range(3):
-                    lam[n, i, j * 8 : j * 8 + 8, quarter * 128 : quarter * 128 + 128] = got2[
-                        pl.ds(unit_base(i, quarter, n, j), 8, stride=2 * SPAN), :
+                for j in range(len(OWNER[n])):
+                    at = EXT * LEVEL0[n] + i * DEEP[n] + j * 8
+                    lam[at : at + 8, quarter * 128 : quarter * 128 + 128] = got2[
+                        pl.ds(unit_base(i, quarter, n, j), 8, stride=2 * SPAN[n]), :
                     ]
         passed[n].start()
-        fields = dot3_nt(split(lam[n].reshape(EXT * DEEP, KEEP)), (zh[...], zl[...]))
-        fields = keep * fields.reshape(EXT, DEEP, LON)
-        deep = pl.ds(n * DEEP, DEEP)
+        rows = lam[EXT * LEVEL0[n] : EXT * (LEVEL0[n] + DEEP[n]), :]
+        fields = dot3_nt(split(rows), (zh[...], zl[...]))
+        fields = keep * fields.reshape(EXT, DEEP[n], LON)
+        deep = pl.ds(LEVEL0[n], DEEP[n])
         force[:, deep, :] = fields - force[:, deep, :]
         edge[n].start()
 
     def adjoint(n):
         edge[n].wait()
-        deep = pl.ds(n * DEEP, DEEP)
+        deep = pl.ds(LEVEL0[n], DEEP[n])
 
         def start(r):
             return force_near[-1 - r, deep, :] if r < 0 else force[r, deep, :]
@@ -535,9 +551,9 @@
 
     def finish(n):
         passed[n].wait()
-        deep = pl.ds(n * DEEP, DEEP)
-        fields = dot3_nt(split(lam_near[n].reshape(ROWS * DEEP, KEEP)), (zh[...], zl[...]))
-        fields = fields.reshape(ROWS, DEEP, LON)
+        deep = pl.ds(LEVEL0[n], DEEP[n])
+        rows = lam_near[ROWS * LEVEL0[n] : ROWS * (LEVEL0[n] + DEEP[n]), :]
+        fields = dot3_nt(split(rows), (zh[...], zl[...])).reshape(ROWS, DEEP[n], LON)
         for i in range(ROWS):
             out[src(i), deep, :] = fields[i] - p[i, deep, :]
 
@@ -583,8 +599,8 @@
     f32 = jnp.float32
     sems = pltpu.SemaphoreType.DMA
     scratch = [
-        ((CHUNKS, ROWS, DEEP, KEEP), f32),
-        ((CHUNKS, ROWS, DEEP, KEEP), f32),
+        ((ROWS * LEV, KEEP), f32),
+        ((ROWS * LEV, KEEP), f32),
         ((2, LEV, LON), f32),
         ((8, LON), f32),
         ((8, LON), f32),
@@ -598,13 +614,12 @@
         ((4, 2, 2, 8, NLAT), f32),
         ((EXT, LEV, LON), f32),
         ((EXT, LEV, LON), f32),
-        ((EXT, LEV, KEEP), f32),
-        ((CHUNKS * PART, 128), f32),
-        ((CHUNKS * PART, 128), f32),
+        ((BLOCKS, 128), f32),
+        ((BLOCKS, 128), f32),
         ((LON, 2 * SLOTS), jnp.bfloat16),
         ((CELL_ROWS, 2 * SLOTS), jnp.bfloat16),
-        ((CHUNKS, EXT, DEEP, KEEP), f32),
-        ((CHUNKS, ROWS, DEEP, KEEP), f32),
+        ((EXT * LEV, KEEP), f32),
+        ((ROWS * LEV, KEEP), f32),
         ((EXT, LEV, LON), f32),
         ((2, LEV, LON), f32),
     ]
@@ -632,7 +647,7 @@
         scratch_shapes=[pltpu.VMEM(shape, kind) for shape, kind in scratch]
         + [sems((MISC,)), sems((MISC,)), sems((8,)), sems((8,))]
         + [sems((CHUNKS,))] * 4
-        + [pltpu.VMEM((CHUNKS * PART, 128), f32)] * 2,
+        + [pltpu.VMEM((BLOCKS, 128), f32)] * 2,
         compiler_params=pltpu.CompilerParams(
             vmem_limit_bytes=VMEM_LIMIT, collective_id=0, has_side_effects=True
         ),

time: 313 us -> 312 us (level)
  no operation moved by 1% of the time
where the time goes in v4:
time: 312 us; the launch traced here: 311 us
  Pallas kernels  308 us (99%)
    pallas_call x1, Pallas kernels, body(): pl.pallas_call(kernel, out_shape=jax.ShapeDtypeStruct((ROWS, LEV, LON), f...  308 us

profile of v4, /device:TPU:1, one launch (start us, length us, event | category | flops | bytes accessed | tf_op | source)
XLA Modules:
  0.0 311.0 jit_solution(1440410444386164506)
XLA Ops:
  0.7 307.9 %shard_map.154 = f32[6,72,768]{2,1,0:T(8,128)} custom-call(f32[6,72,768]{2,1,0:T(8,128)} %bitcast.11, f32[6,72,768]{2,1,0:T(8,128)} %bitcast.12, f32[6,1,768]{2,1,0:T(1,128)} %bitcast.13, f32[6,1,768]{2,1,0:T(1,128)} %bitcast.14, f32[6,1,768]{2,1,0:T(1,128)} %bitcast.15, f32[8,384]{1,0:T(8,128)} %spectrum.1, s32[1,512]{1,0:T(1,128)} %cells.1, ...), custom_call_target="tpu_custom_call" | custom-call | tf_op jit(solution)/shard_map/pallas_call | solution.py:642
  308.5 2.5 copy.19

commit v5 on v4

--- a/solution.py
+++ b/solution.py
@@ -165,6 +165,13 @@
     outer = me + 2 * core - 1
     before = (win + NWIN - 1) % NWIN
     after = (win + 1) % NWIN
+    is_first, is_last = 1 - (win + NWIN - 1) // NWIN, (win + 1) // NWIN
+    mirror = me + 2 - 4 * half
+    before_tile = me + is_first * (2 - 4 * half)
+    after_tile = me + is_last * (2 - 4 * half)
+
+    def rows_at(t):
+        return t + is_last * (2 - 4 * ((t // 2) % 2))
 
     def copy(src, dst, ssem, rsem, window, tile):
         return pltpu.make_async_remote_copy(
@@ -190,9 +197,9 @@
         )
         return carry
 
-    for window in (before, after):
+    for neighbour in ((before, before_tile), (after, after_tile)):
         pl.semaphore_signal(
-            barrier, inc=1, device_id=(window, me), device_id_type=pl.DeviceIdType.MESH
+            barrier, inc=1, device_id=neighbour, device_id_type=pl.DeviceIdType.MESH
         )
     lax.fori_loop(1, TILES, greet, 0)
 
@@ -239,13 +246,13 @@
         return ref.at[pl.ds(ROWS * LEVEL0[n], ROWS * DEEP[n]), :]
 
     shift = [
-        misc(SHIFT + n, six(coefs, n), six(shifted, n), before, me) for n in range(CHUNKS)
+        misc(SHIFT + n, six(coefs, n), six(shifted, n), before, before_tile) for n in range(CHUNKS)
     ]
     pack_inner = misc(PACK_IN, pack, pack_in, win, partner)
     pack_outer = misc(PACK_OUT, pack, pack_out, win, outer)
     cells_outer = misc(OBS, obs, obs_far, win, outer)
     spec_across = misc(
-        SPEC, spec.at[xx, half, core], spec.at[xx, half, core], win, me + 2 - 4 * half
+        SPEC, spec.at[xx, half, core], spec.at[xx, half, core], win, mirror
     )
     rim = (1 - core) * (ROWS - 2)
     halo = misc(HALO, inc.at[pl.ds(rim, 2)], near, win, partner)
@@ -348,12 +355,12 @@
 
     def fwd(n, d, rows):
         return copy(
-            block(send, n, d, rows), block(got, n, me, rows), fwd_s.at[n], fwd_r.at[n], win, d
+            block(send, n, d, rows), block(got, n, rows_at(me), rows), fwd_s.at[n], fwd_r.at[n], win, d
         )
 
     def bwd(n, d, rows):
         return copy(
-            block(send2, n, d, rows), block(got2, n, me, rows), bwd_s.at[n], bwd_r.at[n], win, d
+            block(send2, n, rows_at(d), rows), block(got2, n, me, rows), bwd_s.at[n], bwd_r.at[n], win, d
         )
 
     def total(ref, ref2, ssem, rsem, n, rows):
@@ -370,13 +377,13 @@
 
         lax.fori_loop(0, 16, one, 0)
 
-    def own_block(n):
-        return pl.ds(PART0[n] + me * SPAN[n], SPAN[n])
+    def own_block(n, t):
+        return pl.ds(PART0[n] + t * SPAN[n], SPAN[n])
 
     def send_fwd(n):
         for there in (0, 1):
             all_tiles(lambda d: fwd(n, d, rows_of(n, there)).start(), there)
-        got[own_block(n), :] = send[own_block(n), :]
+        got[own_block(n, rows_at(me)), :] = send[own_block(n, me), :]
 
     def send_bwd(n):
         for mine in (0, 1):
@@ -386,7 +393,7 @@
                 for there in (0, 1):
                     all_tiles(lambda d: bwd(n, d, rows_of(n, mine)).start(), there)
 
-        got2[own_block(n), :] = send2[own_block(n), :]
+        got2[own_block(n, me), :] = send2[own_block(n, rows_at(me)), :]
 
     def by_core(act):
         for mine in (0, 1):
@@ -505,7 +512,7 @@
             lam.at[pl.ds(EXT * LEVEL0[n], ROWS * DEEP[n]), :],
             six(lam_near, n),
             after,
-            me,
+            after_tile,
         )
         for n in range(CHUNKS)
     ]

time: 312 us -> 305 us (0.978)
  Pallas kernels: 308 us -> 301 us
    pallas_call x1, Pallas kernels: 308 us -> 301 us  [body(): pl.pallas_call(kernel, out_shape=jax.ShapeDtypeStruct((ROWS, LEV, LON), f...]
where the time goes in v5:
time: 305 us; the launch traced here: 304 us
  Pallas kernels  301 us (99%)
    pallas_call x1, Pallas kernels, body(): pl.pallas_call(kernel, out_shape=jax.ShapeDtypeStruct((ROWS, LEV, LON), f...  301 us

profile of v5, /device:TPU:1, one launch (start us, length us, event | category | flops | bytes accessed | tf_op | source)
XLA Modules:
  0.0 304.4 jit_solution(12482356906762336413)
XLA Ops:
  0.7 301.3 %shard_map.154 = f32[6,72,768]{2,1,0:T(8,128)} custom-call(f32[6,72,768]{2,1,0:T(8,128)} %bitcast.11, f32[6,72,768]{2,1,0:T(8,128)} %bitcast.12, f32[6,1,768]{2,1,0:T(1,128)} %bitcast.13, f32[6,1,768]{2,1,0:T(1,128)} %bitcast.14, f32[6,1,768]{2,1,0:T(1,128)} %bitcast.15, f32[8,384]{1,0:T(8,128)} %spectrum.1, s32[1,512]{1,0:T(1,128)} %cells.1, ...), custom_call_target="tpu_custom_call" | custom-call | tf_op jit(solution)/shard_map/pallas_call | solution.py:649
  301.9 2.5 copy.19
